TPU v7x, 32 devices: a whole 2x2x4 slice. The times are simulated.
32 devices in a mesh: row: 4 (over y, core), col: 8 (over z, x).
Axes of the slice: x: 2, y: 2, z: 4, core: 2. Of those that a mesh axis runs over, the one named last changes fastest.
Arguments:
- features: bfloat16 [16384, 256], P(('col', 'row')), may hold values from -6 to 6
- weight: bfloat16 [256, 256], replicated, may hold values from -0.375 to 0.375
- tile_coords: int32 [4, 8, 144, 2], P('row', 'col'), may hold values from 0 to 31, as said below
- tile_live: int32 [4, 8], P('row', 'col'), may hold values from 36 to 144, as said below
- tile_edges: int32 [4, 8, 144, 128, 128], P('row', 'col'), may hold values 0 or 1
- row_degree: int32 [16384], P(('row', 'col')), may hold values from 1 to 64
- col_degree: int32 [16384], P(('col', 'row')), may hold values from 1 to 64
- cotangent: bfloat16 [16384, 256], P(('row', 'col')), may hold values from -6 to 6
Outputs:
- aggregated: bfloat16 [16384, 256], P(('row', 'col'))
- grad_features: bfloat16 [16384, 256], P(('col', 'row'))
- grad_weight: float32 [256, 256], replicated
Inputs may be any that keep to these rules, and one draw needn't show every extreme that they name: `tile_coords`: entry 0 of a slot is a row tile of the block, 0 to 31, entry 1 a column tile, 0 to 15; slots naming the same position add. `tile_live`: the number of live leading slots of each block's list; some block fills all 144 slots.
All inputs are finite; a program needn't handle non-finite values. No bound on the sum of `tile_edges` on one device may be relied on, other than what follows from the above.
Results may differ from a plain program's by a relative error of at most 0.0055.
Values may be sent and summed in bfloat16 or wider, within the bound.
A program may use at most 128 MiB of HBM per device.

v0:
```python
import jax
import jax.numpy as jnp
from jax import lax
from jax.sharding import PartitionSpec as P


def tile_products(
    local_edges, source_tiles, source_index, target_index, target_tiles, flipped, valid_slots
):
    weighted = jnp.where(valid_slots[:, None, None], local_edges, 0).astype(jnp.bfloat16)
    picked = jnp.take(source_tiles, source_index, axis=0)
    pattern = "sji,sjf->sif" if flipped else "sij,sjf->sif"
    products = jnp.einsum(pattern, weighted, picked, preferred_element_type=jnp.float32)
    empty = jnp.zeros((target_tiles, products.shape[1], products.shape[2]), jnp.float32)
    totals = empty.at[target_index].add(products)
    return totals.reshape(target_tiles, -1)


def aggregate(
    local_edges, live_count, source_tiles, source_index, target_index, target_tiles, flipped
):
    slots = local_edges.shape[0]
    tile_size = local_edges.shape[1]
    width = source_tiles.shape[2]
    valid_slots = jnp.arange(slots, dtype=jnp.int32) < live_count
    totals = tile_products(
        local_edges, source_tiles, source_index, target_index, target_tiles, flipped, valid_slots
    )
    return totals.reshape(target_tiles * tile_size, width)


def shards(features, weight, tile_coords, tile_live, tile_edges, row_degree, col_degree, cotangent):
    tile_size = tile_edges.shape[-1]
    width = features.shape[1]
    row_scale = lax.rsqrt(row_degree.astype(jnp.float32))
    col_scale = lax.rsqrt(col_degree.astype(jnp.float32))
    coords = tile_coords[0, 0]
    live_count = tile_live[0, 0]
    local_edges = tile_edges[0, 0]
    row_index = coords[:, 0]
    col_index = coords[:, 1]
    own_panel = (
        col_scale[:, None] * jnp.dot(features, weight, preferred_element_type=jnp.float32)
    ).astype(jnp.bfloat16)
    panel = lax.all_gather(own_panel, "row", axis=0, tiled=True)
    col_tiles = panel.shape[0] // tile_size
    row_tiles = col_tiles * lax.axis_size("col") // lax.axis_size("row")
    partial_value = aggregate(
        local_edges,
        live_count,
        panel.reshape(col_tiles, tile_size, width),
        col_index,
        row_index,
        row_tiles,
        False,
    )
    summed = lax.psum_scatter(partial_value, "col", scatter_dimension=0, tiled=True)
    aggregated = (row_scale[:, None] * summed).astype(jnp.bfloat16)
    upstream = (row_scale[:, None] * cotangent.astype(jnp.float32)).astype(jnp.bfloat16)
    row_panel = lax.all_gather(upstream, "col", axis=0, tiled=True)
    back_partial = aggregate(
        local_edges,
        live_count,
        row_panel.reshape(row_tiles, tile_size, width),
        row_index,
        col_index,
        col_tiles,
        True,
    )
    back_summed = lax.psum_scatter(back_partial, "row", scatter_dimension=0, tiled=True)
    grad_panel = (col_scale[:, None] * back_summed).astype(jnp.bfloat16)
    grad_features = jnp.dot(grad_panel, weight.T, preferred_element_type=jnp.float32).astype(
        jnp.bfloat16
    )
    weight_terms = lax.dot_general(
        features, grad_panel, (((0,), (0,)), ((), ())), preferred_element_type=jnp.float32
    )
    grad_weight = lax.psum(weight_terms, ("row", "col"))
    return (aggregated, grad_features, grad_weight)


def solution(mesh):
    in_specs = (
        P(("col", "row"), None),
        P(),
        P("row", "col", None, None),
        P("row", "col"),
        P("row", "col", None, None, None),
        P(("row", "col")),
        P(("col", "row")),
        P(("row", "col"), None),
    )
    out_specs = (P(("row", "col"), None), P(("col", "row"), None), P())
    return jax.shard_map(shards, mesh=mesh, in_specs=in_specs, out_specs=out_specs, check_vma=False)
```

profile of v0, /device:TPU:0, one launch (start us, length us, event | category | flops | bytes accessed | tf_op | source)
XLA Modules:
  0.0 459.0 jit_solution(7395112142530740836)
XLA Ops:
  7.2 0.0 copy-start
  7.2 0.0 all-gather.3.cloned.1.call-start
  7.2 0.7 convert_rsqrt_fusion
  7.9 0.2 copy-done
  8.1 1.8 fusion.9
  10.0 0.0 all-gather.3.cloned.1.call-update
  10.0 0.0 reduce-scatter.3.cloned.1.call-start
  10.7 0.8 and_reduce_fusion.1
  11.5 18.1 %all-gather.3.cloned.1.call-done = bf16[2048,256]{1,0:T(8,128)(2,1)} async-done(((bf16[512,256]{1,0:T(8,128)(2,1)}), bf16[2048,256]{1,0:T(8,128)(2,1)}) %all-gather.3.cloned.1.call-update) | async-done | bytes 1048592 | tf_op jit(solution)/shard_map/all_gather | solution.py:45
  29.6 8.5 %gather_fusion = bf16[144,128,256]{2,1,0:T(8,128)(2,1)} fusion(bf16[16,128,256]{2,1,0:T(8,128)(2,1)} %bitcast.23, s32[1024]{0:T(1024)S(1)} %pad_clamp_fusion.1), kind=kCustom, calls=%fused_computation | custom fusion | bytes 18874944 | tf_op jit(solution)/shard_map/jit(_take)/gather | solution.py:11
  38.1 15.6 %fusion.3 = f32[144,128,256]{2,1,0:T(8,128)} fusion(bf16[144,128,256]{2,1,0:T(8,128)(2,1)} %gather_fusion, pred[144]{0:T(512)(128)(4,1)S(1)} %get-tuple-element.8, s32[1,1,144,128,128]{4,3,2,1,0:T(8,128)} %param.12, pred[144]{0:T(512)(128)(4,1)S(1)} %iota_compare_fusion), kind=kOutput, calls=%fused_computation.8 | convolution fusion | flops 1217396736 | bytes 37749024 | tf_op jit(solution)/shard_map/sij,sjf->sif/dot_general | solution.py:13
  53.7 2.5 broadcast_in_dim.48
  56.2 0.0 copy-start.4
  56.2 0.0 copy-start.3
  56.2 42.7 %scatter_fusion = f32[32,128,256]{2,1,0:T(8,128)} fusion(f32[32,128,256]{2,1,0:T(8,128)} %broadcast_in_dim.48, s32[144]{0:T(256)S(1)} %bitcast.27, f32[144,128,256]{2,1,0:T(8,128)} %fusion.3), kind=kCustom, calls=%fused_computation.2 | custom fusion | flops 4718592 | bytes 56623680 | tf_op jit(solution)/shard_map/scatter-add | solution.py:15
  98.9 0.0 reduce-scatter.3.cloned.1.call-update
  99.0 0.0 all-gather.5.cloned.1.call-start
  99.0 0.0 copy-done.4
  99.0 88.5 %reduce-scatter.3.cloned.1.call-done = f32[512,256]{1,0:T(8,128)} async-done(((f32[4096,256]{1,0:T(8,128)}), f32[512,256]{1,0:T(8,128)}) %reduce-scatter.3.cloned.1.call-update) | async-done | bytes 524304 | tf_op jit(solution)/shard_map/reduce_scatter | solution.py:57
  187.6 0.0 copy-done.3
  187.6 2.0 multiply_convert_fusion.1
  189.6 0.0 all-gather.5.cloned.1.call-update
  189.6 0.0 reduce-scatter.5.cloned.1.call-start
  189.6 50.0 %all-gather.5.cloned.1.call-done = bf16[4096,256]{1,0:T(8,128)(2,1)} async-done(((bf16[512,256]{1,0:T(8,128)(2,1)}), bf16[4096,256]{1,0:T(8,128)(2,1)}) %all-gather.5.cloned.1.call-update) | async-done | bytes 2097168 | tf_op jit(solution)/shard_map/all_gather | solution.py:60
  239.6 8.9 %gather_fusion.1 = bf16[144,128,256]{2,1,0:T(8,128)(2,1)} fusion(bf16[32,128,256]{2,1,0:T(8,128)(2,1)} %bitcast.24, s32[1024]{0:T(1024)S(1)} %pad_clamp_fusion), kind=kCustom, calls=%fused_computation.1 | custom fusion | bytes 18874944 | tf_op jit(solution)/shard_map/jit(_take)/gather | solution.py:11
  248.5 12.2 %fusion.1 = f32[144,128,256]{2,1,0:T(8,128)} fusion(bf16[144,128,256]{2,1,0:T(8,128)(2,1)} %gather_fusion.1, pred[144]{0:T(512)(128)(4,1)S(1)} %get-tuple-element.12, s32[1,1,144,128,128]{4,3,2,1,0:T(8,128)} %param.12, pred[144]{0:T(512)(128)(4,1)S(1)} %iota_compare_fusion), kind=kOutput, calls=%fused_computation.6 | convolution fusion | flops 1217396736 | bytes 37749024 | tf_op jit(solution)/shard_map/sji,sjf->sif/dot_general | solution.py:13
  260.8 0.2 broadcast_in_dim.53
  261.0 0.0 copy-start.2
  261.0 27.3 %scatter_fusion.1 = f32[16,128,256]{2,1,0:T(8,128)S(1)} fusion(f32[16,128,256]{2,1,0:T(8,128)S(1)} %broadcast_in_dim.53, s32[144]{0:T(256)S(1)} %bitcast.26, f32[144,128,256]{2,1,0:T(8,128)} %fusion.1), kind=kCustom, calls=%fused_computation.3 | custom fusion | flops 4718592 | bytes 56623680 | tf_op jit(solution)/shard_map/scatter-add | solution.py:15
  288.3 0.0 copy-start.1
  288.3 1.3 copy-done.1
  289.6 0.0 reduce-scatter.5.cloned.1.call-update
  289.7 0.0 all-reduce.2.cloned.1.call-start
  289.7 30.1 %reduce-scatter.5.cloned.1.call-done = f32[512,256]{1,0:T(8,128)} async-done(((f32[2048,256]{1,0:T(8,128)}), f32[512,256]{1,0:T(8,128)}) %reduce-scatter.5.cloned.1.call-update) | async-done | bytes 524304 | tf_op jit(solution)/shard_map/reduce_scatter | solution.py:70
  319.8 2.1 convolution_bitcast_fusion
  321.9 0.0 all-reduce.2.cloned.1.call-update
  321.9 0.0 copy-done.2
  321.9 2.0 convolution_convert_fusion
  323.9 126.8 %all-reduce.2.cloned.1.call-done = f32[256,256]{0,1:T(8,128)} async-done(((f32[256,256]{0,1:T(8,128)}), f32[256,256]{0,1:T(8,128)}) %all-reduce.2.cloned.1.call-update) | async-done | bytes 262160 | tf_op jit(solution)/shard_map/psum | solution.py:78
  450.7 1.8 copy.12
  (4 shorter events, 0.0 us)
Async XLA Ops:
  7.2 1.0 copy-start
  7.2 22.4 %all-gather.3.cloned.1.call-start = ((), (), s32[]{:S(2)}) async-start(), calls=%async_computation.2 | async-start | bytes 1310720 | tf_op jit(solution)/shard_map/all_gather | solution.py:45
  10.0 177.6 %reduce-scatter.3.cloned.1.call-start = ((), (), s32[]{:S(2)}) async-start(), calls=%async_computation.3 | async-start | bytes 4718592 | tf_op jit(solution)/shard_map/reduce_scatter | solution.py:57
  56.2 42.8 %copy-start.4 = (s32[512]{0:T(512)S(1)}, s32[512]{0:T(512)}, u32[]{:S(2)}) copy-start(s32[512]{0:T(512)} %param.13) | copy-start | bytes 6148
  56.2 131.4 %copy-start.3 = (bf16[512,256]{1,0:T(8,128)(2,1)S(1)}, bf16[512,256]{1,0:T(8,128)(2,1)}, u32[]{:S(2)}) copy-start(bf16[512,256]{1,0:T(8,128)(2,1)} %param.15) | copy-start | bytes 786436
  99.0 140.6 %all-gather.5.cloned.1.call-start = ((), (), s32[]{:S(2)}) async-start(), calls=%async_computation.4 | async-start | bytes 2359296 | tf_op jit(solution)/shard_map/all_gather | solution.py:60
  189.6 130.2 %reduce-scatter.5.cloned.1.call-start = ((), (), s32[]{:S(2)}) async-start(), calls=%async_computation.5 | async-start | bytes 2621440 | tf_op jit(solution)/shard_map/reduce_scatter | solution.py:70
  261.0 60.9 %copy-start.2 = (bf16[256,256]{1,0:T(8,128)(2,1)S(1)}, bf16[256,256]{1,0:T(8,128)(2,1)}, u32[]{:S(2)}) copy-start(bf16[256,256]{1,0:T(8,128)(2,1)} %param.9) | copy-start | bytes 393220
  288.3 1.3 copy-start.1
  289.7 161.1 %all-reduce.2.cloned.1.call-start = ((), (), s32[]{:S(2)}) async-start(), calls=%async_computation.6 | async-start | bytes 524288 | tf_op jit(solution)/shard_map/psum | solution.py:78
Sparse Core Ops, SparseCore 0:
  10.1 19.4 all-gather.2
  99.1 88.4 reduce-scatter.2
  190.5 49.0 all-gather.4
  289.8 29.9 reduce-scatter.4
  325.7 124.9 all-reduce.1
where the time goes:
time: 460 us; the launch traced here: 459 us
  waiting for transfers between devices  314 us (68%)
  other arithmetic  73.5 us (16%)
  matrix products  33.8 us (7%)
  local copies, waits for them, and re-layouts  23.5 us (5%)
  between operations  14.5 us (3%)
    psum x1, waiting for transfers between devices, shards(): grad_weight = lax.psum(weight_terms, ('row', 'col'))  127 us
    reduce_scatter x1, waiting for transfers between devices, shards(): lax.psum_scatter(partial_value, 'col', scatter_dimension=0, tiled=True)  88.5 us
    scatter-add x2, other arithmetic, tile_products(): totals = empty.at[target_index].add(products)  70 us
    all_gather x1, waiting for transfers between devices, shards(): row_panel = lax.all_gather(upstream, 'col', axis=0, tiled=True)  50 us
    reduce_scatter x1, waiting for transfers between devices, shards(): lax.psum_scatter(back_partial, 'row', scatter_dimension=0, tiled=True)  30.1 us
    dot_general x2, matrix products, tile_products(): jnp.einsum(pattern, weighted, picked, preferred_element_type=jnp.float32)  27.8 us
    all_gather x1, waiting for transfers between devices, shards(): panel = lax.all_gather(own_panel, 'row', axis=0, tiled=True)  18.1 us
    gather x2, local copies, waits for them, and re-layouts, tile_products(): picked = jnp.take(source_tiles, source_index, axis=0)  17.5 us
  transfers between devices with their start and end apart: 5, of which 5 were waited for; matrix products, arithmetic and copies ran while one was open for 1% of the time, Pallas kernels for 0%

commit v1 on v0

v1 whole, which is shorter than its diff:
```python
import functools

import jax
import jax.numpy as jnp
from jax import lax
from jax.experimental import pallas as pl
from jax.experimental.pallas import tpu as pltpu
from jax.sharding import PartitionSpec as P

MESH = pl.DeviceIdType.MESH
CORES = 2
SLOW = 4
MB = 1024 * 1024


def greet(n_row, n_col, row, col):
    barrier = pltpu.get_barrier_semaphore()
    for k in range(1, n_row):
        peer = lax.rem(row + k, n_row)
        pl.semaphore_signal(barrier, inc=1, device_id=(peer, col), device_id_type=MESH)
    for k in range(1, n_col):
        peer = lax.rem(col + k, n_col)
        pl.semaphore_signal(barrier, inc=1, device_id=(row, peer), device_id_type=MESH)
    pl.semaphore_wait(barrier, n_row + n_col - 2)


def remote(src, dst, send, recv, target):
    return pltpu.make_async_remote_copy(
        src_ref=src,
        dst_ref=dst,
        send_sem=send,
        recv_sem=recv,
        device_id=target,
        device_id_type=MESH,
    )


def gather_kernel(
    n_row, n_col, feat, weight, col_scale, cot, row_scale, panel, upstream, p_send, p_recv, u_send, u_recv
):
    row = lax.axis_index("row")
    col = lax.axis_index("col")
    n_y = n_row // CORES
    n_fast = n_col // SLOW
    y, core = row // CORES, lax.rem(row, CORES)
    z, x = col // n_fast, lax.rem(col, n_fast)
    upstream[pl.ds(col, 1)] = (row_scale[...] * cot[...].astype(jnp.float32)).astype(jnp.bfloat16)[None]
    greet(n_row, n_col, row, col)

    def up_copy(slot, send, target):
        return remote(upstream.at[slot], upstream.at[slot], u_send.at[send], u_recv.at[slot], (row, target))

    def fan_fast(slot, base):
        for k in range(1, n_fast):
            up_copy(slot, base + k - 1, z * n_fast + lax.rem(x + k, n_fast)).start()

    def fan_fast_wait(slot, base):
        for k in range(1, n_fast):
            up_copy(slot, base + k - 1, z * n_fast + lax.rem(x + k, n_fast)).wait_send()

    per = n_fast
    up_ok, down_ok = z + 1 < SLOW, z >= 1

    @pl.when(up_ok)
    def _():
        up_copy(col, 0, col + n_fast).start()

    @pl.when(down_ok)
    def _():
        up_copy(col, 1, col - n_fast).start()

    fan_fast(col, 2)

    own = jnp.dot(feat[...], weight[...], preferred_element_type=jnp.float32)
    panel[pl.ds(row, 1)] = (col_scale[...] * own).astype(jnp.bfloat16)[None]

    def p_copy(slot, send, target):
        return remote(panel.at[slot], panel.at[slot], p_send.at[send], p_recv.at[slot], (target, col))

    other = y * CORES + (1 - core)
    for k in range(1, n_y):
        p_copy(row, k, lax.rem(y + k, n_y) * CORES + core).start()
    p_copy(row, 0, other).start()

    base = 2 + n_fast - 1
    for t in range(1, SLOW):
        for side in range(2):
            first = base + ((t - 1) * 2 + side) * per
            if side == 0:
                here, slot = z >= t, col - t * n_fast
                onward, target = up_ok, col + n_fast
            else:
                here, slot = z + t < SLOW, col + t * n_fast
                onward, target = down_ok, col - n_fast

            @pl.when(here)
            def _():
                up_copy(slot, first, col).wait_recv()

                @pl.when(onward)
                def _():
                    up_copy(slot, first, target).start()

                fan_fast(slot, first + 1)

        if t == 1:
            for k in range(1, n_y):
                slot = lax.rem(y + k, n_y) * CORES + core
                p_copy(slot, n_y - 1 + k, other).wait_recv()
                p_copy(slot, n_y - 1 + k, other).start()

    for k in range(n_y):
        slot = lax.rem(y + k, n_y) * CORES + (1 - core)
        p_copy(slot, 0, other).wait_recv()
    for k in range(1, n_fast):
        for t in range(SLOW):
            slot = t * n_fast + lax.rem(x + k, n_fast)
            up_copy(slot, 0, col).wait_recv()

    p_copy(row, 0, other).wait_send()
    for k in range(1, n_y):
        p_copy(row, k, other).wait_send()
        p_copy(row, n_y - 1 + k, other).wait_send()

    @pl.when(up_ok)
    def _():
        up_copy(col, 0, col).wait_send()

    @pl.when(down_ok)
    def _():
        up_copy(col, 1, col).wait_send()

    fan_fast_wait(col, 2)
    for t in range(1, SLOW):
        for side in range(2):
            first = base + ((t - 1) * 2 + side) * per
            if side == 0:
                here, onward = z >= t, up_ok
            else:
                here, onward = z + t < SLOW, down_ok

            @pl.when(here)
            def _():
                @pl.when(onward)
                def _():
                    up_copy(col, first, col).wait_send()

                fan_fast_wait(col, first + 1)


def tile_kernel(steps, group, coords, live, edges, panel, upstream, out, back, acc, back_acc):
    step = pl.program_id(0)
    row_tiles, col_tiles = out.shape[0], back.shape[0]

    @pl.when(step == 0)
    def _():
        acc[...] = jnp.zeros_like(acc)
        back_acc[...] = jnp.zeros_like(back_acc)

    unroll = 8 if group % 8 == 0 else 1

    def body(i, carry):
        for j in range(unroll):
            local = i * unroll + j
            slot = step * group + local
            r, c = coords[2 * slot], coords[2 * slot + 1]
            ok = slot < live[0]
            r_to = jnp.where(ok, r, row_tiles)
            c_to = jnp.where(ok, c, col_tiles)
            tile = edges[local].astype(jnp.float32).astype(jnp.bfloat16)
            acc[r_to] += jnp.dot(tile, panel[c], preferred_element_type=jnp.float32)
            back_acc[c_to] += lax.dot_general(
                tile, upstream[r], (((0,), (0,)), ((), ())), preferred_element_type=jnp.float32
            )
        return carry

    lax.fori_loop(0, group // unroll, body, 0)

    @pl.when(step == steps - 1)
    def _():
        out[...] = acc[:row_tiles].astype(jnp.bfloat16)
        back[...] = back_acc[:col_tiles].astype(jnp.bfloat16)


def scatter_kernel(
    n_row,
    n_col,
    part,
    back,
    feat,
    weight,
    row_scale,
    col_scale,
    out,
    grad_feat,
    grad_weight,
    x_buf,
    z_out,
    z_buf,
    c_buf,
    y_out,
    y_buf,
    w_out,
    w1_buf,
    q_out,
    w2_buf,
    q_all,
    w4_buf,
    x_send,
    x_recv,
    z_send,
    z_recv,
    c_send,
    c_recv,
    y_send,
    y_recv,
    w_send,
    w1_recv,
    w2_recv,
    w3_recv,
    w4_recv,
):
    row = lax.axis_index("row")
    col = lax.axis_index("col")
    n_y = n_row // CORES
    n_fast = n_col // SLOW
    y, core = row // CORES, lax.rem(row, CORES)
    z, x = col // n_fast, lax.rem(col, n_fast)
    f32, bf16 = jnp.float32, jnp.bfloat16
    other = y * CORES + (1 - core)
    greet(n_row, n_col, row, col)

    def c_copy(k):
        block = lax.rem(y + k, n_y) * CORES + (1 - core)
        return remote(back.at[block], c_buf.at[k], c_send.at[k], c_recv.at[k], (other, col))

    for k in reversed(range(n_y)):
        c_copy(k).start()

    def x_copy(t, k):
        to = lax.rem(x + k, n_fast)
        block = lax.rem(z + t, SLOW) * n_fast + to
        slot = t * (n_fast - 1) + k - 1
        return remote(
            part.at[block], x_buf.at[slot], x_send.at[slot], x_recv.at[slot], (row, z * n_fast + to)
        )

    order = (2, 3, 1, 0)
    for t in order:
        for k in range(1, n_fast):
            x_copy(t, k).start()

    def y_copy(k):
        return remote(
            y_out.at[k],
            y_buf.at[k],
            y_send.at[k],
            y_recv.at[k],
            (lax.rem(y + k, n_y) * CORES + core, col),
        )

    own_back = None
    for k in reversed(range(n_y)):
        c_copy(k).wait_recv()
        block = lax.rem(y + k, n_y) * CORES + core
        total = back[pl.ds(block, 1)][0].astype(f32) + c_buf[k].astype(f32)
        if k:
            y_out[k] = total.astype(bf16)
            y_copy(k).start()
        else:
            y_out[0] = total.astype(bf16)

    def z_copy(t):
        return remote(
            z_out.at[t],
            z_buf.at[t],
            z_send.at[t],
            z_recv.at[t],
            (row, lax.rem(z + t, SLOW) * n_fast + x),
        )

    def merge_x(t):
        block = lax.rem(z + t, SLOW) * n_fast + x
        total = part[pl.ds(block, 1)][0].astype(f32)
        for k in range(1, n_fast):
            x_copy(t, k).wait_recv()
            total = total + x_buf[t * (n_fast - 1) + k - 1].astype(f32)
        z_out[t] = total.astype(bf16)
        if t:
            z_copy(t).start()

    merge_x(order[0])

    total = y_out[0].astype(f32)
    for k in range(1, n_y):
        y_copy(k).wait_recv()
        total = total + y_buf[k].astype(f32)
    grad_panel = (col_scale[...] * total).astype(bf16)
    terms = lax.dot_general(feat[...], grad_panel, (((0,), (0,)), ((), ())), preferred_element_type=f32)
    quarter = terms.shape[0] // n_row
    piece = quarter // n_col
    for r in range(n_row):
        w_out[r] = terms[r * quarter : (r + 1) * quarter]

    def w1_copy(k):
        to = lax.rem(row + k, n_row)
        return remote(w_out.at[to], w1_buf.at[k], w_send.at[k], w1_recv.at[k], (to, col))

    for k in range(1, n_row):
        w1_copy(k).start()
    grad_feat[...] = lax.dot_general(
        grad_panel, weight[...], (((1,), (1,)), ((), ())), preferred_element_type=f32
    ).astype(bf16)

    merge_x(order[1])

    total = w_out[pl.ds(row, 1)][0]
    for k in range(1, n_row):
        w1_copy(k).wait_recv()
        total = total + w1_buf[k]
    for j in range(n_col):
        q_out[j] = total[j * piece : (j + 1) * piece]

    def w2_copy(k):
        to = lax.rem(col + k, n_col)
        return remote(q_out.at[to], w2_buf.at[k], w_send.at[n_row + k], w2_recv.at[k], (row, to))

    for k in range(1, n_col):
        w2_copy(k).start()

    merge_x(order[2])

    total = q_out[pl.ds(col, 1)][0]
    for k in range(1, n_col):
        w2_copy(k).wait_recv()
        total = total + w2_buf[k]
    q_all[pl.ds(col, 1)] = total[None]

    def w3_copy(k):
        to = lax.rem(col + k, n_col)
        return remote(
            q_all.at[col], q_all.at[col], w_send.at[n_row + n_col + k], w3_recv.at[k], (row, to)
        )

    for k in range(1, n_col):
        w3_copy(k).start()

    merge_x(order[3])

    for k in range(1, n_col):
        w3_copy(k).wait_recv()
    for j in range(n_col):
        w4_buf[pl.ds(row, 1), j * piece : (j + 1) * piece] = q_all[j][None]

    def w4_copy(k):
        to = lax.rem(row + k, n_row)
        return remote(
            w4_buf.at[row], w4_buf.at[row], w_send.at[n_row + 2 * n_col + k], w4_recv.at[k], (to, col)
        )

    for k in range(1, n_row):
        w4_copy(k).start()

    total = z_out[0].astype(f32)
    for t in order[:3]:
        z_copy(t).wait_recv()
        total = total + z_buf[t].astype(f32)
    out[...] = (row_scale[...] * total).astype(bf16)

    for k in range(1, n_row):
        w4_copy(k).wait_recv()
    for r in range(n_row):
        grad_weight[r * quarter : (r + 1) * quarter] = w4_buf[r]

    for k in range(n_y):
        c_copy(k).wait_send()
        if k:
            y_copy(k).wait_send()
    for t in range(SLOW):
        for k in range(1, n_fast):
            x_copy(t, k).wait_send()
        if t:
            z_copy(t).wait_send()
    for k in range(1, n_row):
        w1_copy(k).wait_send()
        w4_copy(k).wait_send()
    for k in range(1, n_col):
        w2_copy(k).wait_send()
        w3_copy(k).wait_send()


def vmem(n):
    return [pl.BlockSpec(memory_space=pltpu.VMEM)] * n


def shards(
    n_row, n_col, features, weight, tile_coords, tile_live, tile_edges, row_degree, col_degree, cotangent
):
    f32, bf16 = jnp.float32, jnp.bfloat16
    dma, shape = pltpu.SemaphoreType.DMA, jax.ShapeDtypeStruct
    tile = tile_edges.shape[-1]
    slots = tile_edges.shape[2]
    nodes, width = features.shape
    n_y, n_fast = n_row // CORES, n_col // SLOW
    row_scale = lax.rsqrt(row_degree.astype(f32))[:, None]
    col_scale = lax.rsqrt(col_degree.astype(f32))[:, None]

    panel, upstream = pl.pallas_call(
        functools.partial(gather_kernel, n_row, n_col),
        out_shape=(shape((n_row, nodes, width), bf16), shape((n_col, nodes, width), bf16)),
        in_specs=vmem(5),
        out_specs=tuple(vmem(2)),
        scratch_shapes=[
            dma((2 * n_y,)),
            dma((n_row,)),
            dma((2 + n_fast - 1 + 2 * (SLOW - 1) * n_fast,)),
            dma((n_col,)),
        ],
        compiler_params=pltpu.CompilerParams(
            collective_id=0, has_side_effects=True, vmem_limit_bytes=40 * MB
        ),
        name="gather",
    )(features, weight, col_scale, cotangent, row_scale)

    col_tiles = n_row * nodes // tile
    row_tiles = n_col * nodes // tile
    group = max(g for g in range(1, 25) if slots % g == 0)
    steps = slots // group
    part, back = pl.pallas_call(
        functools.partial(tile_kernel, steps, group),
        out_shape=(shape((row_tiles, tile, width), bf16), shape((col_tiles, tile, width), bf16)),
        grid_spec=pltpu.PrefetchScalarGridSpec(
            num_scalar_prefetch=2,
            grid=(steps,),
            in_specs=[
                pl.BlockSpec((group, tile, tile), lambda i, *_: (i, 0, 0)),
                pl.BlockSpec(memory_space=pltpu.VMEM),
                pl.BlockSpec(memory_space=pltpu.VMEM),
            ],
            out_specs=(
                pl.BlockSpec((row_tiles, tile, width), lambda i, *_: (0, 0, 0)),
                pl.BlockSpec((col_tiles, tile, width), lambda i, *_: (0, 0, 0)),
            ),
            scratch_shapes=[
                pltpu.VMEM((row_tiles + 1, tile, width), f32),
                pltpu.VMEM((col_tiles + 1, tile, width), f32),
            ],
        ),
        compiler_params=pltpu.CompilerParams(vmem_limit_bytes=48 * MB),
        name="tiles",
    )(
        tile_coords.reshape(-1),
        tile_live.reshape(-1),
        tile_edges[0, 0],
        panel.reshape(col_tiles, tile, width),
        upstream.reshape(row_tiles, tile, width),
    )

    quarter = width // n_row
    piece = quarter // n_col
    block = (nodes, width)
    return pl.pallas_call(
        functools.partial(scatter_kernel, n_row, n_col),
        out_shape=(shape(block, bf16), shape(block, bf16), shape((width, width), f32)),
        in_specs=vmem(6),
        out_specs=tuple(vmem(3)),
        scratch_shapes=[
            pltpu.VMEM((SLOW * (n_fast - 1),) + block, bf16),
            pltpu.VMEM((SLOW,) + block, bf16),
            pltpu.VMEM((SLOW,) + block, bf16),
            pltpu.VMEM((n_y,) + block, bf16),
            pltpu.VMEM((n_y,) + block, bf16),
            pltpu.VMEM((n_y,) + block, bf16),
            pltpu.VMEM((n_row, quarter, width), f32),
            pltpu.VMEM((n_row, quarter, width), f32),
            pltpu.VMEM((n_col, piece, width), f32),
            pltpu.VMEM((n_col, piece, width), f32),
            pltpu.VMEM((n_col, piece, width), f32),
            pltpu.VMEM((n_row, quarter, width), f32),
            dma((SLOW * (n_fast - 1),)),
            dma((SLOW * (n_fast - 1),)),
            dma((SLOW,)),
            dma((SLOW,)),
            dma((n_y,)),
            dma((n_y,)),
            dma((n_y,)),
            dma((n_y,)),
            dma((2 * n_row + 2 * n_col,)),
            dma((n_row,)),
            dma((n_col,)),
            dma((n_col,)),
            dma((n_row,)),
        ],
        compiler_params=pltpu.CompilerParams(
            collective_id=1, has_side_effects=True, vmem_limit_bytes=56 * MB
        ),
        name="scatter",
    )(
        part.reshape((n_col,) + block),
        back.reshape((n_row,) + block),
        features,
        weight,
        row_scale,
        col_scale,
    )


def solution(mesh):
    in_specs = (
        P(("col", "row"), None),
        P(),
        P("row", "col", None, None),
        P("row", "col"),
        P("row", "col", None, None, None),
        P(("row", "col")),
        P(("col", "row")),
        P(("row", "col"), None),
    )
    out_specs = (P(("row", "col"), None), P(("col", "row"), None), P())
    body = functools.partial(shards, mesh.shape["row"], mesh.shape["col"])
    return jax.shard_map(body, mesh=mesh, in_specs=in_specs, out_specs=out_specs, check_vma=False)
```

time: 460 us -> 102 us (0.22)
  waiting for transfers between devices: 314 us -> 0 us
  Pallas kernels: 0 us -> 86 us
  other arithmetic: 73.5 us -> 1.37 us
  matrix products: 33.8 us -> 0 us
  between operations: 14.5 us -> 1.38 us
  local copies, waits for them, and re-layouts: 23.5 us -> 12.7 us
    psum x1 -> x0, waiting for transfers between devices: 127 us -> none  [shards(): grad_weight = lax.psum(weight_terms, ('row', 'col'))]
    reduce_scatter x2 -> x0, waiting for transfers between devices: 119 us -> none  [the longest x1 88.5 us: shards(): lax.psum_scatter(partial_value, 'col', scatter_dimension=0, tiled=True)]
    pallas_call x0 -> x3, Pallas kernels: none -> 86 us  [the longest x1 41.5 us: shards(): pl.pallas_call(functools.partial(scatter_kernel, n_row, n_col), out_shape...]
    scatter-add x2 -> x0, other arithmetic: 70 us -> none  [tile_products(): totals = empty.at[target_index].add(products)]
    all_gather x2 -> x0, waiting for transfers between devices: 68.1 us -> none  [the longest x1 50 us: shards(): row_panel = lax.all_gather(upstream, 'col', axis=0, tiled=True)]
    dot_general x5 -> x0, matrix products: 33.8 us -> none  [the longest x2 27.8 us: tile_products(): jnp.einsum(pattern, weighted, picked, preferred_element_type=jnp.float32)]
    gather x2 -> x0, local copies, waits for them, and re-layouts: 17.5 us -> none  [tile_products(): picked = jnp.take(source_tiles, source_index, axis=0)]
    unnamed x11 -> x20, local copies, waits for them, and re-layouts: 3.32 us -> 12.2 us
  transfers between devices with their start and end apart: 5 -> 0, of which waited for: 5 -> 0; matrix products, arithmetic and copies ran while one was open for 1% -> 0% of each run, Pallas kernels for 0% -> 0%
where the time goes in v1:
time: 102 us; the launch traced here: 101 us
  Pallas kernels  86 us (84%)
  local copies, waits for them, and re-layouts  12.7 us (12%)
  between operations  1.38 us (1%)
  other arithmetic  1.37 us (1%)
    pallas_call x1, Pallas kernels, shards(): pl.pallas_call(functools.partial(scatter_kernel, n_row, n_col), out_shape...  41.5 us
    pallas_call x1, Pallas kernels, shards(): pl.pallas_call(functools.partial(gather_kernel, n_row, n_col), out_shape=...  32.7 us
    unnamed x20, local copies, waits for them, and re-layouts  12.2 us
    pallas_call x1, Pallas kernels, shards(): pl.pallas_call(functools.partial(tile_kernel, steps, group), out_shape=(s...  11.7 us

profile of v1, /device:TPU:0, one launch (start us, length us, event | category | flops | bytes accessed | tf_op | source)
XLA Modules:
  0.0 101.4 jit_solution(18395753812229579709)
XLA Ops:
  1.3 0.7 convert_rsqrt_fusion
  2.0 0.7 convert_rsqrt_fusion.1
  2.7 0.8 copy.11
  3.4 0.1 reshape.24.coords
  3.6 0.1 copy.12.col_scale
  3.7 0.0 copy-start
  3.8 0.1 copy.13.row_scale
  3.9 0.0 copy-start.4
  3.9 0.9 copy-done.4
  4.9 0.0 copy-start.6
  4.9 0.9 copy-done.6
  5.8 0.0 copy-start.7
  5.8 0.9 copy-done.7
  6.7 0.0 copy-start.1
  6.7 32.7 %gather.1 = (bf16[4,512,256]{2,1,0:T(8,128)(2,1)S(1)}, bf16[8,512,256]{2,1,0:T(8,128)(2,1)S(1)}) custom-call(bf16[512,256]{1,0:T(8,128)(2,1)S(1)} %copy-done.4, bf16[256,256]{1,0:T(8,128)(2,1)S(1)} %copy-done.6, f32[512,1]{1,0:T(8,128)S(1)} %copy.12.col_scale, bf16[512,256]{1,0:T(8,128)(2,1)S(1)} %copy-done.7, f32[512,1]{1,0:T(8,128)S(1)} %copy.13.row_scale), custom_call_target="tpu_custom_call" | custom-call | tf_op jit(solution)/shard_map/gather/pallas_call | solution.py:408
  39.5 0.0 copy-start.3
  39.5 1.3 %copy-done.3 = bf16[8,512,256]{2,1,0:T(8,128)(2,1)} copy-done((bf16[8,512,256]{2,1,0:T(8,128)(2,1)}, bf16[8,512,256]{2,1,0:T(8,128)(2,1)S(1)}, u32[]{:S(2)}) %copy-start.3) | copy-done | bytes 2097176
  40.8 11.7 %tiles.1 = (bf16[32,128,256]{2,1,0:T(8,128)(2,1)S(1)}, bf16[16,128,256]{2,1,0:T(8,128)(2,1)S(1)}) custom-call(s32[288]{0:T(512)S(1)} %reshape.24.coords, s32[1]{0:T(128)} %bitcast.10.live, s32[144,128,128]{2,1,0:T(8,128)} %bitcast.15, bf16[16,128,256]{2,1,0:T(8,128)(2,1)S(1)} %bitcast.14, bf16[32,128,256]{2,1,0:T(8,128)(2,1)} %bitcast.12), custom_call_target="tpu_custom_call" | custom-call | tf_op jit(solution)/shard_map/tiles/pallas_call | solution.py:429
  52.5 0.0 copy-done
  52.5 0.0 copy-done.1
  52.5 0.0 copy-start.2
  52.5 1.3 %copy-done.2 = bf16[32,128,256]{2,1,0:T(8,128)(2,1)} copy-done((bf16[32,128,256]{2,1,0:T(8,128)(2,1)}, bf16[32,128,256]{2,1,0:T(8,128)(2,1)S(1)}, u32[]{:S(2)}) %copy-start.2) | copy-done | bytes 2097176
  53.9 0.0 copy-start.5
  53.9 1.0 copy-done.5
  54.9 41.5 %scatter.1 = (bf16[512,256]{1,0:T(8,128)(2,1)}, bf16[512,256]{1,0:T(8,128)(2,1)}, f32[256,256]{1,0:T(8,128)}) custom-call(bf16[8,512,256]{2,1,0:T(8,128)(2,1)} %bitcast.11, bf16[4,512,256]{2,1,0:T(8,128)(2,1)} %bitcast.13, bf16[512,256]{1,0:T(8,128)(2,1)} %feat.3, bf16[256,256]{1,0:T(8,128)(2,1)} %weight.3, f32[512,1]{1,0:T(8,128)} %copy-done.1, ...), custom_call_target="tpu_custom_call" | custom-call | tf_op jit(solution)/shard_map/scatter/pallas_call | solution.py:462
  96.4 1.7 %copy.20 = bf16[512,256]{1,0:T(8,128)(2,1)} copy(bf16[512,256]{1,0:T(8,128)(2,1)} %get-tuple-element.14) | data formatting | bytes 524288
  98.1 1.7 %copy.21 = bf16[512,256]{1,0:T(8,128)(2,1)} copy(bf16[512,256]{1,0:T(8,128)(2,1)} %get-tuple-element.15) | data formatting | bytes 524288
  99.8 1.7 %copy.22 = f32[256,256]{1,0:T(8,128)} copy(f32[256,256]{1,0:T(8,128)} %get-tuple-element.16) | data formatting | bytes 524288
Async XLA Ops:
  3.7 48.8 %copy-start = (f32[512,1]{1,0:T(8,128)}, f32[512,1]{1,0:T(8,128)S(1)}, u32[]{:S(2)}) copy-start(f32[512,1]{1,0:T(8,128)S(1)} %copy.12.col_scale) | copy-start | bytes 6148
  3.9 1.0 copy-start.4
  4.9 0.9 copy-start.6
  5.8 0.9 copy-start.7
  6.7 45.8 %copy-start.1 = (f32[512,1]{1,0:T(8,128)}, f32[512,1]{1,0:T(8,128)S(1)}, u32[]{:S(2)}) copy-start(f32[512,1]{1,0:T(8,128)S(1)} %copy.13.row_scale) | copy-start | bytes 6148
  39.5 1.3 %copy-start.3 = (bf16[8,512,256]{2,1,0:T(8,128)(2,1)}, bf16[8,512,256]{2,1,0:T(8,128)(2,1)S(1)}, u32[]{:S(2)}) copy-start(bf16[8,512,256]{2,1,0:T(8,128)(2,1)S(1)} %get-tuple-element.8) | copy-start | bytes 6291460
  52.5 1.3 %copy-start.2 = (bf16[32,128,256]{2,1,0:T(8,128)(2,1)}, bf16[32,128,256]{2,1,0:T(8,128)(2,1)S(1)}, u32[]{:S(2)}) copy-start(bf16[32,128,256]{2,1,0:T(8,128)(2,1)S(1)} %get-tuple-element.9) | copy-start | bytes 6291460
  53.9 1.0 copy-start.5

commit v2 on v1

v2 whole, which is shorter than its diff:
```python
import functools

import jax
import jax.numpy as jnp
from jax import lax
from jax.experimental import pallas as pl
from jax.experimental.pallas import tpu as pltpu
from jax.sharding import PartitionSpec as P

MESH = pl.DeviceIdType.MESH
CORES = 2
SLOW = 4
MB = 1024 * 1024


def greet(n_row, n_col, row, col):
    barrier = pltpu.get_barrier_semaphore()
    for k in range(1, n_row):
        peer = lax.rem(row + k, n_row)
        pl.semaphore_signal(barrier, inc=1, device_id=(peer, col), device_id_type=MESH)
    for k in range(1, n_col):
        peer = lax.rem(col + k, n_col)
        pl.semaphore_signal(barrier, inc=1, device_id=(row, peer), device_id_type=MESH)
    pl.semaphore_wait(barrier, n_row + n_col - 2)


def remote(src, dst, send, recv, target):
    return pltpu.make_async_remote_copy(
        src_ref=src,
        dst_ref=dst,
        send_sem=send,
        recv_sem=recv,
        device_id=target,
        device_id_type=MESH,
    )


def table_kernel(row_tiles, col_tiles, coords, coords_t, live, tab):
    slots, lanes = coords.shape[0], tab.shape[1]
    count = live[0]
    s_col = lax.broadcasted_iota(jnp.int32, (slots, 1), 0)
    s_row = lax.broadcasted_iota(jnp.int32, (1, lanes), 1)
    place = lax.broadcasted_iota(jnp.int32, (slots, lanes), 1)
    for half, tiles in ((0, row_tiles), (1, col_tiles)):
        key_col = jnp.where(s_col < count, coords[:, half : half + 1], tiles)
        key_row = jnp.where(s_row < count, coords_t[half : half + 1, :], tiles)
        same = (key_row == key_col) & (s_row < s_col)
        earlier = jnp.sum(same.astype(jnp.int32), axis=1, keepdims=True)
        below = jnp.sum((key_row < key_col).astype(jnp.int32), axis=1, keepdims=True)
        chosen = ((earlier + below) == place).astype(jnp.int32)
        source = coords[:, 1 - half : 2 - half]
        follows = (earlier > 0).astype(jnp.int32)
        upto = jnp.sum((key_col <= place).astype(jnp.int32), axis=0, keepdims=True)
        here = jnp.sum((key_col == place).astype(jnp.int32), axis=0, keepdims=True)
        tab[4 * half : 4 * half + 1, :] = jnp.sum(chosen * s_col, axis=0, keepdims=True)
        tab[4 * half + 1 : 4 * half + 2, :] = jnp.sum(chosen * source, axis=0, keepdims=True)
        tab[4 * half + 2 : 4 * half + 3, :] = jnp.sum(chosen * follows, axis=0, keepdims=True)
        tab[4 * half + 3 : 4 * half + 4, :] = jnp.where(here > 0, upto - 1, slots)


def layer_kernel(
    n_row,
    n_col,
    tab,
    feat,
    weight,
    col_scale,
    cot,
    row_scale,
    edges_hbm,
    out,
    grad_feat,
    grad_weight,
    edges,
    panel,
    upstream,
    acc,
    sums,
    part,
    back,
    x_buf,
    z_out,
    z_buf,
    c_buf,
    y_out,
    y_buf,
    w_out,
    w1_buf,
    q_out,
    w2_buf,
    q_all,
    w4_buf,
    e_sem,
    p_send,
    p_recv,
    u_send,
    u_recv,
    x_send,
    x_recv,
    z_send,
    z_recv,
    c_send,
    c_recv,
    y_send,
    y_recv,
    w_send,
    w1_recv,
    w2_recv,
    w3_recv,
    w4_recv,
):
    row = lax.axis_index("row")
    col = lax.axis_index("col")
    n_y = n_row // CORES
    n_fast = n_col // SLOW
    y, core = row // CORES, lax.rem(row, CORES)
    z, x = col // n_fast, lax.rem(col, n_fast)
    f32, bf16 = jnp.float32, jnp.bfloat16
    other = y * CORES + (1 - core)
    slots, tile = edges.shape[0], edges.shape[1]
    tiles_dev = panel.shape[1]
    nodes, width = feat.shape
    block_shape = (tiles_dev, tile, width)

    load_edges = pltpu.make_async_copy(edges_hbm, edges, e_sem)
    load_edges.start()
    own = (row_scale[...] * cot[...].astype(f32)).astype(bf16)
    upstream[pl.ds(col, 1)] = own.reshape((1,) + block_shape)
    greet(n_row, n_col, row, col)

    def up_copy(slot, send, target):
        return remote(upstream.at[slot], upstream.at[slot], u_send.at[send], u_recv.at[slot], (row, target))

    def fan_fast(slot, base):
        for k in range(1, n_fast):
            up_copy(slot, base + k - 1, z * n_fast + lax.rem(x + k, n_fast)).start()

    def fan_fast_wait(slot, base):
        for k in range(1, n_fast):
            up_copy(slot, base + k - 1, z * n_fast + lax.rem(x + k, n_fast)).wait_send()

    up_ok, down_ok = z + 1 < SLOW, z >= 1
    up_base = 2 + n_fast - 1

    @pl.when(up_ok)
    def _():
        up_copy(col, 0, col + n_fast).start()

    @pl.when(down_ok)
    def _():
        up_copy(col, 1, col - n_fast).start()

    fan_fast(col, 2)

    def pass_on(t):
        for side in range(2):
            first = up_base + ((t - 1) * 2 + side) * n_fast
            if side == 0:
                here, slot = z >= t, col - t * n_fast
                onward, target = up_ok, col + n_fast
            else:
                here, slot = z + t < SLOW, col + t * n_fast
                onward, target = down_ok, col - n_fast

            @pl.when(here)
            def _():
                up_copy(slot, first, col).wait_recv()

                @pl.when(onward)
                def _():
                    up_copy(slot, first, target).start()

                fan_fast(slot, first + 1)

    own = jnp.dot(feat[...], weight[...], preferred_element_type=f32)
    panel[pl.ds(row, 1)] = (col_scale[...] * own).astype(bf16).reshape((1,) + block_shape)

    def p_copy(slot, send, target):
        return remote(panel.at[slot], panel.at[slot], p_send.at[send], p_recv.at[slot], (target, col))

    for k in range(1, n_y):
        p_copy(row, k, lax.rem(y + k, n_y) * CORES + core).start()
    p_copy(row, 0, other).start()
    acc[...] = jnp.zeros_like(acc)
    sums[slots] = jnp.zeros((tile, width), bf16)
    for k in range(1, n_y):
        slot = lax.rem(y + k, n_y) * CORES + core
        p_copy(slot, n_y - 1 + k, other).wait_recv()
        p_copy(slot, n_y - 1 + k, other).start()
    pass_on(1)
    for k in range(n_y):
        slot = lax.rem(y + k, n_y) * CORES + (1 - core)
        p_copy(slot, 0, other).wait_recv()
    load_edges.wait()

    unroll = 8 if slots % 16 == 0 else 1

    def products(base, source, flipped, lo, hi):
        def body(i, carry):
            for j in range(unroll):
                n = lo + i * unroll + j
                pick, src = tab[base, n], tab[base + 1, n]
                keep = tab[base + 2, n].astype(f32)
                mat = edges[pick].astype(f32).astype(bf16)
                vals = source[lax.div(src, tiles_dev), lax.rem(src, tiles_dev)]
                dims = (((0,), (0,)), ((), ())) if flipped else (((1,), (0,)), ((), ()))
                total = acc[...] * keep + lax.dot_general(mat, vals, dims, preferred_element_type=f32)
                acc[...] = total
                sums[n] = total.astype(bf16)
            return carry

        lax.fori_loop(0, (hi - lo) // unroll, body, 0)

    half = slots // 2
    products(0, panel, False, 0, half)
    pass_on(2)
    products(0, panel, False, half, slots)
    for block in range(n_col):
        for j in range(tiles_dev):
            part[block, j] = sums[tab[3, block * tiles_dev + j]]

    def x_copy(t, k):
        to = lax.rem(x + k, n_fast)
        block = lax.rem(z + t, SLOW) * n_fast + to
        slot = t * (n_fast - 1) + k - 1
        return remote(
            part.at[block], x_buf.at[slot], x_send.at[slot], x_recv.at[slot], (row, z * n_fast + to)
        )

    order = (2, 3, 1, 0)

    def start_x(i):
        if i >= 2:
            for k in range(1, n_fast):
                x_copy(order[i - 2], k).wait_send()
        for k in range(1, n_fast):
            x_copy(order[i], k).start()

    for t in range(3, SLOW):
        pass_on(t)
    start_x(0)
    start_x(1)

    def z_copy(t):
        return remote(
            z_out.at[t],
            z_buf.at[t],
            z_send.at[t],
            z_recv.at[t],
            (row, lax.rem(z + t, SLOW) * n_fast + x),
        )

    def merge_x(i):
        t = order[i]
        block = lax.rem(z + t, SLOW) * n_fast + x
        total = part[pl.ds(block, 1)][0].astype(f32)
        for k in range(1, n_fast):
            x_copy(t, k).wait_recv()
            total = total + x_buf[t * (n_fast - 1) + k - 1].astype(f32)
        z_out[t] = total.astype(bf16)
        if t:
            z_copy(t).start()

    for k in range(1, n_fast):
        for t in range(SLOW):
            slot = t * n_fast + lax.rem(x + k, n_fast)
            up_copy(slot, 0, col).wait_recv()
    products(4, upstream, True, 0, half)
    merge_x(0)
    start_x(2)
    products(4, upstream, True, half, slots)
    for block in range(n_row):
        for j in range(tiles_dev):
            back[block, j] = sums[tab[7, block * tiles_dev + j]]

    def c_copy(k):
        block = lax.rem(y + k, n_y) * CORES + (1 - core)
        return remote(back.at[block], c_buf.at[k], c_send.at[k], c_recv.at[k], (other, col))

    for k in reversed(range(n_y)):
        c_copy(k).start()

    def y_copy(k):
        return remote(
            y_out.at[k],
            y_buf.at[k],
            y_send.at[k],
            y_recv.at[k],
            (lax.rem(y + k, n_y) * CORES + core, col),
        )

    for k in reversed(range(n_y)):
        c_copy(k).wait_recv()
        block = lax.rem(y + k, n_y) * CORES + core
        total = back[pl.ds(block, 1)][0].astype(f32) + c_buf[k].astype(f32)
        y_out[k] = total.astype(bf16)
        if k:
            y_copy(k).start()

    merge_x(1)
    start_x(3)

    total = y_out[0].astype(f32)
    for k in range(1, n_y):
        y_copy(k).wait_recv()
        total = total + y_buf[k].astype(f32)
    grad_panel = (col_scale[...] * total.reshape((nodes, width))).astype(bf16)
    terms = lax.dot_general(feat[...], grad_panel, (((0,), (0,)), ((), ())), preferred_element_type=f32)
    quarter = width // n_row
    piece = quarter // n_col
    for r in range(n_row):
        w_out[r] = terms[r * quarter : (r + 1) * quarter]

    def w1_copy(k):
        to = lax.rem(row + k, n_row)
        return remote(w_out.at[to], w1_buf.at[k], w_send.at[k], w1_recv.at[k], (to, col))

    for k in range(1, n_row):
        w1_copy(k).start()
    grad_feat[...] = lax.dot_general(
        grad_panel, weight[...], (((1,), (1,)), ((), ())), preferred_element_type=f32
    ).astype(bf16)

    merge_x(2)

    total = w_out[pl.ds(row, 1)][0]
    for k in range(1, n_row):
        w1_copy(k).wait_recv()
        total = total + w1_buf[k]
    for j in range(n_col):
        q_out[j] = total[j * piece : (j + 1) * piece]

    def w2_copy(k):
        to = lax.rem(col + k, n_col)
        return remote(q_out.at[to], w2_buf.at[k], w_send.at[n_row + k], w2_recv.at[k], (row, to))

    for k in range(1, n_col):
        w2_copy(k).start()

    merge_x(3)

    total = q_out[pl.ds(col, 1)][0]
    for k in range(1, n_col):
        w2_copy(k).wait_recv()
        total = total + w2_buf[k]
    q_all[pl.ds(col, 1)] = total[None]

    def w3_copy(k):
        to = lax.rem(col + k, n_col)
        return remote(
            q_all.at[col], q_all.at[col], w_send.at[n_row + n_col + k], w3_recv.at[k], (row, to)
        )

    for k in range(1, n_col):
        w3_copy(k).start()

    total = z_out[0].astype(f32)
    for t in order[:3]:
        z_copy(t).wait_recv()
        total = total + z_buf[t].astype(f32)
    out[...] = (row_scale[...] * total.reshape((nodes, width))).astype(bf16)

    for k in range(1, n_col):
        w3_copy(k).wait_recv()
    for j in range(n_col):
        w4_buf[pl.ds(row, 1), j * piece : (j + 1) * piece] = q_all[j][None]

    def w4_copy(k):
        to = lax.rem(row + k, n_row)
        return remote(
            w4_buf.at[row], w4_buf.at[row], w_send.at[n_row + 2 * n_col + k], w4_recv.at[k], (to, col)
        )

    for k in range(1, n_row):
        w4_copy(k).start()

    p_copy(row, 0, other).wait_send()
    for k in range(1, n_y):
        p_copy(row, k, other).wait_send()
        p_copy(row, n_y - 1 + k, other).wait_send()

    @pl.when(up_ok)
    def _():
        up_copy(col, 0, col).wait_send()

    @pl.when(down_ok)
    def _():
        up_copy(col, 1, col).wait_send()

    fan_fast_wait(col, 2)
    for t in range(1, SLOW):
        for side in range(2):
            first = up_base + ((t - 1) * 2 + side) * n_fast
            if side == 0:
                here, onward = z >= t, up_ok
            else:
                here, onward = z + t < SLOW, down_ok

            @pl.when(here)
            def _():
                @pl.when(onward)
                def _():
                    up_copy(col, first, col).wait_send()

                fan_fast_wait(col, first + 1)

    for k in range(n_y):
        c_copy(k).wait_send()
        if k:
            y_copy(k).wait_send()
    for t in order[2:]:
        for k in range(1, n_fast):
            x_copy(t, k).wait_send()
    for t in order[:3]:
        z_copy(t).wait_send()
    for k in range(1, n_row):
        w1_copy(k).wait_send()
    for k in range(1, n_col):
        w2_copy(k).wait_send()
        w3_copy(k).wait_send()

    for k in range(1, n_row):
        w4_copy(k).wait_recv()
    for r in range(n_row):
        grad_weight[r * quarter : (r + 1) * quarter] = w4_buf[r]
    for k in range(1, n_row):
        w4_copy(k).wait_send()


def vmem(n):
    return [pl.BlockSpec(memory_space=pltpu.VMEM)] * n


def shards(
    n_row, n_col, features, weight, tile_coords, tile_live, tile_edges, row_degree, col_degree, cotangent
):
    f32, bf16 = jnp.float32, jnp.bfloat16
    dma, shape = pltpu.SemaphoreType.DMA, jax.ShapeDtypeStruct
    tile = tile_edges.shape[-1]
    slots = tile_edges.shape[2]
    nodes, width = features.shape
    n_y, n_fast = n_row // CORES, n_col // SLOW
    row_scale = lax.rsqrt(row_degree.astype(f32))[:, None]
    col_scale = lax.rsqrt(col_degree.astype(f32))[:, None]
    tiles_dev = nodes // tile
    col_tiles = n_row * tiles_dev
    row_tiles = n_col * tiles_dev
    lanes = pl.cdiv(max(slots, row_tiles), 128) * 128
    coords = tile_coords[0, 0]
    tab = pl.pallas_call(
        functools.partial(table_kernel, row_tiles, col_tiles),
        out_shape=shape((8, lanes), jnp.int32),
        in_specs=vmem(2) + [pl.BlockSpec(memory_space=pltpu.SMEM)],
        out_specs=pl.BlockSpec(memory_space=pltpu.VMEM),
        name="tables",
    )(coords, jnp.pad(coords.T, ((0, 0), (0, lanes - slots))), tile_live.reshape(-1))

    quarter = width // n_row
    piece = quarter // n_col
    block = (tiles_dev, tile, width)
    return pl.pallas_call(
        functools.partial(layer_kernel, n_row, n_col),
        out_shape=(
            shape((nodes, width), bf16),
            shape((nodes, width), bf16),
            shape((width, width), f32),
        ),
        in_specs=[pl.BlockSpec(memory_space=pltpu.SMEM)]
        + vmem(5)
        + [pl.BlockSpec(memory_space=pl.ANY)],
        out_specs=tuple(vmem(3)),
        scratch_shapes=[
            pltpu.VMEM((slots, tile, tile), jnp.int32),
            pltpu.VMEM((n_row,) + block, bf16),
            pltpu.VMEM((n_col,) + block, bf16),
            pltpu.VMEM((tile, width), f32),
            pltpu.VMEM((slots + 1, tile, width), bf16),
            pltpu.VMEM((n_col,) + block, bf16),
            pltpu.VMEM((n_row,) + block, bf16),
            pltpu.VMEM((SLOW * (n_fast - 1),) + block, bf16),
            pltpu.VMEM((SLOW,) + block, bf16),
            pltpu.VMEM((SLOW,) + block, bf16),
            pltpu.VMEM((n_y,) + block, bf16),
            pltpu.VMEM((n_y,) + block, bf16),
            pltpu.VMEM((n_y,) + block, bf16),
            pltpu.VMEM((n_row, quarter, width), f32),
            pltpu.VMEM((n_row, quarter, width), f32),
            pltpu.VMEM((n_col, piece, width), f32),
            pltpu.VMEM((n_col, piece, width), f32),
            pltpu.VMEM((n_col, piece, width), f32),
            pltpu.VMEM((n_row, quarter, width), f32),
            dma(()),
            dma((2 * n_y,)),
            dma((n_row,)),
            dma((2 + n_fast - 1 + 2 * (SLOW - 1) * n_fast,)),
            dma((n_col,)),
            dma((SLOW * (n_fast - 1),)),
            dma((SLOW * (n_fast - 1),)),
            dma((SLOW,)),
            dma((SLOW,)),
            dma((n_y,)),
            dma((n_y,)),
            dma((n_y,)),
            dma((n_y,)),
            dma((2 * n_row + 2 * n_col,)),
            dma((n_row,)),
            dma((n_col,)),
            dma((n_col,)),
            dma((n_row,)),
        ],
        compiler_params=pltpu.CompilerParams(
            collective_id=0, has_side_effects=True, vmem_limit_bytes=56 * MB
        ),
        name="layer",
    )(tab, features, weight, col_scale, cotangent, row_scale, tile_edges[0, 0])


def solution(mesh):
    in_specs = (
        P(("col", "row"), None),
        P(),
        P("row", "col", None, None),
        P("row", "col"),
        P("row", "col", None, None, None),
        P(("row", "col")),
        P(("col", "row")),
        P(("row", "col"), None),
    )
    out_specs = (P(("row", "col"), None), P(("col", "row"), None), P())
    body = functools.partial(shards, mesh.shape["row"], mesh.shape["col"])
    return jax.shard_map(body, mesh=mesh, in_specs=in_specs, out_specs=out_specs, check_vma=False)
```

time: 102 us -> 87 us (0.85)
  Pallas kernels: 86 us -> 74.4 us
  local copies, waits for them, and re-layouts: 12.7 us -> 9.41 us
    pallas_call x3 -> x2, Pallas kernels: 86 us -> 74.4 us  [the longest x1 72.5 us: shards(): pl.pallas_call(functools.partial(layer_kernel, n_row, n_col), out_shape=(...]
    unnamed x20 -> x3, local copies, waits for them, and re-layouts: 12.2 us -> 5.01 us
    squeeze x0 -> x1, local copies, waits for them, and re-layouts: none -> 1.42 us  [shards(): coords = tile_coords[0, 0]]
    pad x0 -> x1, local copies, waits for them, and re-layouts: none -> 1.27 us  [shards(): jnp.pad(coords.T, ((0, 0), (0, lanes - slots)))]
where the time goes in v2:
time: 87 us; the launch traced here: 86.5 us
  Pallas kernels  74.4 us (86%)
  local copies, waits for them, and re-layouts  9.41 us (11%)
  other arithmetic  1.37 us (2%)
  between operations  1.29 us (1%)
    pallas_call x1, Pallas kernels, shards(): pl.pallas_call(functools.partial(layer_kernel, n_row, n_col), out_shape=(...  72.5 us
    unnamed x3, local copies, waits for them, and re-layouts  5.01 us
    pallas_call x1, Pallas kernels, shards(): pl.pallas_call(functools.partial(table_kernel, row_tiles, col_tiles), out...  1.99 us

profile of v2, /device:TPU:0, one launch (start us, length us, event | category | flops | bytes accessed | tf_op | source)
XLA Modules:
  0.0 86.5 jit_solution(11856458773601958241)
XLA Ops:
  1.3 0.7 convert_rsqrt_fusion
  2.0 0.7 convert_rsqrt_fusion.1
  2.7 1.3 %pad.4.coords_t = s32[2,256]{1,0:T(2,128)} pad(s32[2,144]{1,0:T(2,128)} %bitcast.11, s32[]{:T(128)} %constant.0.clone.1), padding=0_0x0_112 | pad | bytes 3204 | tf_op jit(solution)/shard_map/jit(_pad)/pad | solution.py:456
  3.9 1.4 %copy.12.coords = s32[144,2]{1,0:T(8,128)} copy(s32[144,2]{0,1:T(2,128)} %bitcast.12) | data formatting | bytes 2304 | tf_op jit(solution)/shard_map/squeeze | solution.py:449
  5.3 2.0 %tables.1.tab = s32[8,256]{1,0:T(8,128)} custom-call(s32[144,2]{1,0:T(8,128)} %copy.12.coords, s32[2,256]{1,0:T(2,128)} %pad.4.coords_t, s32[1]{0:T(128)} %bitcast.7.live), custom_call_target="tpu_custom_call" | custom-call | tf_op jit(solution)/shard_map/tables/pallas_call | solution.py:450
  7.3 0.9 copy.13.col_scale
  8.2 0.9 copy.14.row_scale
  9.1 72.5 %layer.1 = (bf16[512,256]{1,0:T(8,128)(2,1)}, bf16[512,256]{1,0:T(8,128)(2,1)}, f32[256,256]{1,0:T(8,128)}) custom-call(s32[8,256]{1,0:T(8,128)} %tables.1.tab, bf16[512,256]{1,0:T(8,128)(2,1)} %feat.1, bf16[256,256]{1,0:T(8,128)(2,1)} %weight.1, f32[512,1]{1,0:T(8,128)} %copy.13.col_scale, bf16[512,256]{1,0:T(8,128)(2,1)} %cot.1, f32[512,1]{1,0:T(8,128)} %copy.14.row_scale, ...), custom_call_target="tpu_custom_call" | custom-call | tf_op jit(solution)/shard_map/layer/pallas_call | solution.py:461
  81.5 1.7 %copy.19 = bf16[512,256]{1,0:T(8,128)(2,1)} copy(bf16[512,256]{1,0:T(8,128)(2,1)} %get-tuple-element.6) | data formatting | bytes 524288
  83.2 1.7 %copy.20 = bf16[512,256]{1,0:T(8,128)(2,1)} copy(bf16[512,256]{1,0:T(8,128)(2,1)} %get-tuple-element.7) | data formatting | bytes 524288
  84.9 1.7 %copy.21 = f32[256,256]{1,0:T(8,128)} copy(f32[256,256]{1,0:T(8,128)} %get-tuple-element.8) | data formatting | bytes 524288

commit v3 on v2

--- a/solution.py
+++ b/solution.py
@@ -35,9 +35,9 @@
     )
 
 
-def table_kernel(row_tiles, col_tiles, coords, coords_t, live, tab):
-    slots, lanes = coords.shape[0], tab.shape[1]
-    count = live[0]
+def fill_tables(row_tiles, col_tiles, packed, turned, count, slots, tab):
+    lanes = tab.shape[1]
+    coords, coords_t = turned[:slots], packed
     s_col = lax.broadcasted_iota(jnp.int32, (slots, 1), 0)
     s_row = lax.broadcasted_iota(jnp.int32, (1, lanes), 1)
     place = lax.broadcasted_iota(jnp.int32, (slots, lanes), 1)
@@ -61,17 +61,21 @@
 def layer_kernel(
     n_row,
     n_col,
-    tab,
+    live,
+    packed,
     feat,
     weight,
-    col_scale,
     cot,
-    row_scale,
     edges_hbm,
     out,
     grad_feat,
     grad_weight,
     edges,
+    turned_edges,
+    tab_vmem,
+    tab,
+    row_scale,
+    col_scale,
     panel,
     upstream,
     acc,
@@ -91,6 +95,7 @@
     q_all,
     w4_buf,
     e_sem,
+    t_sem,
     p_send,
     p_recv,
     u_send,
@@ -124,6 +129,14 @@
 
     load_edges = pltpu.make_async_copy(edges_hbm, edges, e_sem)
     load_edges.start()
+    table = packed[...]
+    turned = jnp.transpose(table)
+    lanes = table.shape[1]
+    for h in range(nodes // lanes):
+        at = slice(h * lanes, (h + 1) * lanes)
+        row_scale[at, :] = lax.rsqrt(turned[:, 2 + h : 3 + h].astype(f32))
+        first = 2 + nodes // lanes + h
+        col_scale[at, :] = lax.rsqrt(turned[:, first : first + 1].astype(f32))
     own = (row_scale[...] * cot[...].astype(f32)).astype(bf16)
     upstream[pl.ds(col, 1)] = own.reshape((1,) + block_shape)
     greet(n_row, n_col, row, col)
@@ -181,6 +194,9 @@
     for k in range(1, n_y):
         p_copy(row, k, lax.rem(y + k, n_y) * CORES + core).start()
     p_copy(row, 0, other).start()
+    fill_tables(n_col * tiles_dev, n_row * tiles_dev, table, turned, live[0], slots, tab_vmem)
+    load_tab = pltpu.make_async_copy(tab_vmem, tab, t_sem)
+    load_tab.start()
     acc[...] = jnp.zeros_like(acc)
     sums[slots] = jnp.zeros((tile, width), bf16)
     for k in range(1, n_y):
@@ -192,6 +208,7 @@
         slot = lax.rem(y + k, n_y) * CORES + (1 - core)
         p_copy(slot, 0, other).wait_recv()
     load_edges.wait()
+    load_tab.wait()
 
     unroll = 8 if slots % 16 == 0 else 1
 
@@ -201,10 +218,9 @@
                 n = lo + i * unroll + j
                 pick, src = tab[base, n], tab[base + 1, n]
                 keep = tab[base + 2, n].astype(f32)
-                mat = edges[pick].astype(f32).astype(bf16)
+                mat = turned_edges[pick] if flipped else edges[pick].astype(f32).astype(bf16)
                 vals = source[lax.div(src, tiles_dev), lax.rem(src, tiles_dev)]
-                dims = (((0,), (0,)), ((), ())) if flipped else (((1,), (0,)), ((), ()))
-                total = acc[...] * keep + lax.dot_general(mat, vals, dims, preferred_element_type=f32)
+                total = acc[...] * keep + jnp.dot(mat, vals, preferred_element_type=f32)
                 acc[...] = total
                 sums[n] = total.astype(bf16)
             return carry
@@ -238,8 +254,14 @@
 
     for t in range(3, SLOW):
         pass_on(t)
-    start_x(0)
-    start_x(1)
+
+    def turn(i, carry):
+        for j in range(unroll):
+            n = i * unroll + j
+            turned_edges[n] = jnp.transpose(edges[n].astype(f32)).astype(bf16)
+        return carry
+
+    lax.fori_loop(0, slots // unroll, turn, 0)
 
     def z_copy(t):
         return remote(
@@ -265,6 +287,8 @@
         for t in range(SLOW):
             slot = t * n_fast + lax.rem(x + k, n_fast)
             up_copy(slot, 0, col).wait_recv()
+    start_x(0)
+    start_x(1)
     products(4, upstream, True, 0, half)
     merge_x(0)
     start_x(2)
@@ -427,6 +451,15 @@
         w4_copy(k).wait_send()
 
 
+def hand_over_kernel(a, b, c, a_out, b_out, c_out, sems):
+    pairs = ((a, a_out), (b, b_out), (c, c_out))
+    copies = [pltpu.make_async_copy(src, dst, sems.at[i]) for i, (src, dst) in enumerate(pairs)]
+    for copy in copies:
+        copy.start()
+    for copy in copies:
+        copy.wait()
+
+
 def vmem(n):
     return [pl.BlockSpec(memory_space=pltpu.VMEM)] * n
 
@@ -440,25 +473,18 @@
     slots = tile_edges.shape[2]
     nodes, width = features.shape
     n_y, n_fast = n_row // CORES, n_col // SLOW
-    row_scale = lax.rsqrt(row_degree.astype(f32))[:, None]
-    col_scale = lax.rsqrt(col_degree.astype(f32))[:, None]
     tiles_dev = nodes // tile
-    col_tiles = n_row * tiles_dev
     row_tiles = n_col * tiles_dev
     lanes = pl.cdiv(max(slots, row_tiles), 128) * 128
-    coords = tile_coords[0, 0]
-    tab = pl.pallas_call(
-        functools.partial(table_kernel, row_tiles, col_tiles),
-        out_shape=shape((8, lanes), jnp.int32),
-        in_specs=vmem(2) + [pl.BlockSpec(memory_space=pltpu.SMEM)],
-        out_specs=pl.BlockSpec(memory_space=pltpu.VMEM),
-        name="tables",
-    )(coords, jnp.pad(coords.T, ((0, 0), (0, lanes - slots))), tile_live.reshape(-1))
+    coords = jnp.pad(tile_coords[0, 0].T, ((0, 0), (0, lanes - slots)))
+    degrees = [row_degree.reshape(-1, lanes), col_degree.reshape(-1, lanes)]
+    used = 2 + 2 * degrees[0].shape[0]
+    packed = jnp.pad(jnp.concatenate([coords] + degrees), ((0, -used % 8), (0, 0)))
 
     quarter = width // n_row
     piece = quarter // n_col
     block = (tiles_dev, tile, width)
-    return pl.pallas_call(
+    results = pl.pallas_call(
         functools.partial(layer_kernel, n_row, n_col),
         out_shape=(
             shape((nodes, width), bf16),
@@ -466,11 +492,16 @@
             shape((width, width), f32),
         ),
         in_specs=[pl.BlockSpec(memory_space=pltpu.SMEM)]
-        + vmem(5)
+        + vmem(4)
         + [pl.BlockSpec(memory_space=pl.ANY)],
         out_specs=tuple(vmem(3)),
         scratch_shapes=[
             pltpu.VMEM((slots, tile, tile), jnp.int32),
+            pltpu.VMEM((slots, tile, tile), bf16),
+            pltpu.VMEM((8, lanes), jnp.int32),
+            pltpu.SMEM((8, lanes), jnp.int32),
+            pltpu.VMEM((nodes, 1), f32),
+            pltpu.VMEM((nodes, 1), f32),
             pltpu.VMEM((n_row,) + block, bf16),
             pltpu.VMEM((n_col,) + block, bf16),
             pltpu.VMEM((tile, width), f32),
@@ -489,6 +520,7 @@
             pltpu.VMEM((n_col, piece, width), f32),
             pltpu.VMEM((n_col, piece, width), f32),
             pltpu.VMEM((n_row, quarter, width), f32),
+            dma(()),
             dma(()),
             dma((2 * n_y,)),
             dma((n_row,)),
@@ -512,7 +544,16 @@
             collective_id=0, has_side_effects=True, vmem_limit_bytes=56 * MB
         ),
         name="layer",
-    )(tab, features, weight, col_scale, cotangent, row_scale, tile_edges[0, 0])
+    )(tile_live.reshape(-1), packed, features, weight, cotangent, tile_edges[0, 0])
+    return pl.pallas_call(
+        hand_over_kernel,
+        out_shape=tuple(shape(r.shape, r.dtype) for r in results),
+        in_specs=[pl.BlockSpec(memory_space=pl.ANY)] * 3,
+        out_specs=tuple([pl.BlockSpec(memory_space=pl.ANY)] * 3),
+        scratch_shapes=[dma((3,))],
+        compiler_params=pltpu.CompilerParams(vmem_limit_bytes=60 * MB),
+        name="hand_over",
+    )(*results)
 
 
 def solution(mesh):

time: 87 us -> 102 us (1.17)
  Pallas kernels: 74.4 us -> 98 us
  local copies, waits for them, and re-layouts: 9.41 us -> 1.99 us
    pallas_call x1, Pallas kernels: 1.99 us -> 25 us  [shards(): pl.pallas_call(hand_over_kernel, out_shape=tuple((shape(r.shape, r.dtype)...]
    unnamed x3 -> x0, local copies, waits for them, and re-layouts: 5.01 us -> none
    broadcast_in_dim x2 -> x0, local copies, waits for them, and re-layouts: 1.72 us -> none  [the longest x1 0.86 us: shards(): col_scale = lax.rsqrt(col_degree.astype(f32))[:, None]]
    squeeze x1 -> x0, local copies, waits for them, and re-layouts: 1.42 us -> none  [shards(): coords = tile_coords[0, 0]]
    reshape x0 -> x2, local copies, waits for them, and re-layouts: none -> 1.39 us  [shards(): degrees = [row_degree.reshape(-1, lanes), col_degree.reshape(-1, lanes)]]
    rsqrt x2 -> x0, other arithmetic: 1.37 us -> none  [the longest x1 0.69 us: shards(): col_scale = lax.rsqrt(col_degree.astype(f32))[:, None]]
where the time goes in v3:
time: 102 us
  Pallas kernels  98 us (96%)
  local copies, waits for them, and re-layouts  1.99 us (2%)
  between operations  1.29 us (1%)
    pallas_call x1, Pallas kernels, shards(): pl.pallas_call(functools.partial(layer_kernel, n_row, n_col), out_shape=(...  73 us
    pallas_call x1, Pallas kernels, shards(): pl.pallas_call(hand_over_kernel, out_shape=tuple((shape(r.shape, r.dtype)...  25 us

profile of v3, /device:TPU:0, one launch (start us, length us, event | category | flops | bytes accessed | tf_op | source)
XLA Modules:
  0.0 101.9 jit_solution(8502970751647444805)
XLA Ops:
  1.3 0.7 reshape.16
  2.0 0.7 reshape.17
  2.7 0.7 fusion
  3.4 0.6 pad.9.packed
  4.0 73.0 %layer.1 = (bf16[512,256]{1,0:T(8,128)(2,1)}, bf16[512,256]{1,0:T(8,128)(2,1)}, f32[256,256]{1,0:T(8,128)}) custom-call(s32[1]{0:T(128)} %bitcast.5.live, s32[8,256]{1,0:T(8,128)} %pad.9.packed, bf16[512,256]{1,0:T(8,128)(2,1)} %feat.1, bf16[256,256]{1,0:T(8,128)(2,1)} %weight.1, bf16[512,256]{1,0:T(8,128)(2,1)} %cot.1, s32[144,128,128]{2,1,0:T(8,128)} %bitcast.6), custom_call_target="tpu_custom_call" | custom-call | tf_op jit(solution)/shard_map/layer/pallas_call | solution.py:487
  77.0 25.0 %hand_over.1 = (bf16[512,256]{1,0:T(8,128)(2,1)}, bf16[512,256]{1,0:T(8,128)(2,1)}, f32[256,256]{1,0:T(8,128)}) custom-call(bf16[512,256]{1,0:T(8,128)(2,1)} %get-tuple-element.6.a, bf16[512,256]{1,0:T(8,128)(2,1)} %get-tuple-element.7.b, f32[256,256]{1,0:T(8,128)} %get-tuple-element.8.c), custom_call_target="tpu_custom_call" | custom-call | tf_op jit(solution)/shard_map/hand_over/pallas_call | solution.py:548

commit v4 on v3

--- a/solution.py
+++ b/solution.py
@@ -62,7 +62,9 @@
     n_row,
     n_col,
     live,
-    packed,
+    coords,
+    row_degree,
+    col_degree,
     feat,
     weight,
     cot,
@@ -72,11 +74,13 @@
     grad_weight,
     edges,
     turned_edges,
+    packed,
     tab_vmem,
     tab,
     row_scale,
     col_scale,
     panel,
+    turned_feat,
     upstream,
     acc,
     sums,
@@ -98,6 +102,8 @@
     t_sem,
     p_send,
     p_recv,
+    f_send,
+    f_recv,
     u_send,
     u_recv,
     x_send,
@@ -129,13 +135,18 @@
 
     load_edges = pltpu.make_async_copy(edges_hbm, edges, e_sem)
     load_edges.start()
+    lanes = row_degree.shape[1]
+    parts = nodes // lanes
+    packed[...] = jnp.zeros_like(packed)
+    packed[0:2, :slots] = coords[...]
+    packed[2 : 2 + parts] = row_degree[...]
+    packed[2 + parts : 2 + 2 * parts] = col_degree[...]
     table = packed[...]
     turned = jnp.transpose(table)
-    lanes = table.shape[1]
-    for h in range(nodes // lanes):
+    for h in range(parts):
         at = slice(h * lanes, (h + 1) * lanes)
         row_scale[at, :] = lax.rsqrt(turned[:, 2 + h : 3 + h].astype(f32))
-        first = 2 + nodes // lanes + h
+        first = 2 + parts + h
         col_scale[at, :] = lax.rsqrt(turned[:, first : first + 1].astype(f32))
     own = (row_scale[...] * cot[...].astype(f32)).astype(bf16)
     upstream[pl.ds(col, 1)] = own.reshape((1,) + block_shape)
@@ -194,6 +205,18 @@
     for k in range(1, n_y):
         p_copy(row, k, lax.rem(y + k, n_y) * CORES + core).start()
     p_copy(row, 0, other).start()
+
+    scaled = jnp.transpose(col_scale[...] * feat[...].astype(f32))
+    turned_feat[pl.ds(row, 1)] = scaled.astype(bf16)[None]
+
+    def f_copy(slot, send, target):
+        return remote(
+            turned_feat.at[slot], turned_feat.at[slot], f_send.at[send], f_recv.at[slot], (target, col)
+        )
+
+    for k in range(1, n_y):
+        f_copy(row, k, lax.rem(y + k, n_y) * CORES + core).start()
+    f_copy(row, 0, other).start()
     fill_tables(n_col * tiles_dev, n_row * tiles_dev, table, turned, live[0], slots, tab_vmem)
     load_tab = pltpu.make_async_copy(tab_vmem, tab, t_sem)
     load_tab.start()
@@ -230,6 +253,10 @@
     half = slots // 2
     products(0, panel, False, 0, half)
     pass_on(2)
+    for k in range(1, n_y):
+        slot = lax.rem(y + k, n_y) * CORES + core
+        f_copy(slot, n_y - 1 + k, other).wait_recv()
+        f_copy(slot, n_y - 1 + k, other).start()
     products(0, panel, False, half, slots)
     for block in range(n_col):
         for j in range(tiles_dev):
@@ -288,10 +315,8 @@
             slot = t * n_fast + lax.rem(x + k, n_fast)
             up_copy(slot, 0, col).wait_recv()
     start_x(0)
+    products(4, upstream, True, 0, half)
     start_x(1)
-    products(4, upstream, True, 0, half)
-    merge_x(0)
-    start_x(2)
     products(4, upstream, True, half, slots)
     for block in range(n_row):
         for j in range(tiles_dev):
@@ -303,6 +328,26 @@
 
     for k in reversed(range(n_y)):
         c_copy(k).start()
+
+    for k in range(n_y):
+        slot = lax.rem(y + k, n_y) * CORES + (1 - core)
+        f_copy(slot, 0, other).wait_recv()
+    quarter = width // n_row
+    piece = quarter // n_col
+    terms = jnp.zeros((width, width), f32)
+    for block in range(n_row):
+        terms = terms + jnp.dot(
+            turned_feat[block], back[block].reshape((nodes, width)), preferred_element_type=f32
+        )
+    for r in range(n_row):
+        w_out[r] = terms[r * quarter : (r + 1) * quarter]
+
+    def w1_copy(k):
+        to = lax.rem(row + k, n_row)
+        return remote(w_out.at[to], w1_buf.at[k], w_send.at[k], w1_recv.at[k], (to, col))
+
+    for k in range(1, n_row):
+        w1_copy(k).start()
 
     def y_copy(k):
         return remote(
@@ -321,31 +366,8 @@
         if k:
             y_copy(k).start()
 
-    merge_x(1)
-    start_x(3)
-
-    total = y_out[0].astype(f32)
-    for k in range(1, n_y):
-        y_copy(k).wait_recv()
-        total = total + y_buf[k].astype(f32)
-    grad_panel = (col_scale[...] * total.reshape((nodes, width))).astype(bf16)
-    terms = lax.dot_general(feat[...], grad_panel, (((0,), (0,)), ((), ())), preferred_element_type=f32)
-    quarter = width // n_row
-    piece = quarter // n_col
-    for r in range(n_row):
-        w_out[r] = terms[r * quarter : (r + 1) * quarter]
-
-    def w1_copy(k):
-        to = lax.rem(row + k, n_row)
-        return remote(w_out.at[to], w1_buf.at[k], w_send.at[k], w1_recv.at[k], (to, col))
-
-    for k in range(1, n_row):
-        w1_copy(k).start()
-    grad_feat[...] = lax.dot_general(
-        grad_panel, weight[...], (((1,), (1,)), ((), ())), preferred_element_type=f32
-    ).astype(bf16)
-
-    merge_x(2)
+    merge_x(0)
+    start_x(2)
 
     total = w_out[pl.ds(row, 1)][0]
     for k in range(1, n_row):
@@ -361,7 +383,17 @@
     for k in range(1, n_col):
         w2_copy(k).start()
 
-    merge_x(3)
+    merge_x(1)
+    start_x(3)
+
+    total = y_out[0].astype(f32)
+    for k in range(1, n_y):
+        y_copy(k).wait_recv()
+        total = total + y_buf[k].astype(f32)
+    grad_panel = (col_scale[...] * total.reshape((nodes, width))).astype(bf16)
+    grad_feat[...] = lax.dot_general(
+        grad_panel, weight[...], (((1,), (1,)), ((), ())), preferred_element_type=f32
+    ).astype(bf16)
 
     total = q_out[pl.ds(col, 1)][0]
     for k in range(1, n_col):
@@ -378,28 +410,35 @@
     for k in range(1, n_col):
         w3_copy(k).start()
 
+    merge_x(2)
+
+    for k in range(1, n_col):
+        w3_copy(k).wait_recv()
+    for j in range(n_col):
+        w4_buf[pl.ds(row, 1), j * piece : (j + 1) * piece] = q_all[j][None]
+
+    def w4_copy(k):
+        to = lax.rem(row + k, n_row)
+        return remote(
+            w4_buf.at[row], w4_buf.at[row], w_send.at[n_row + 2 * n_col + k], w4_recv.at[k], (to, col)
+        )
+
+    for k in range(1, n_row):
+        w4_copy(k).start()
+
+    merge_x(3)
+
     total = z_out[0].astype(f32)
     for t in order[:3]:
         z_copy(t).wait_recv()
         total = total + z_buf[t].astype(f32)
     out[...] = (row_scale[...] * total.reshape((nodes, width))).astype(bf16)
 
-    for k in range(1, n_col):
-        w3_copy(k).wait_recv()
-    for j in range(n_col):
-        w4_buf[pl.ds(row, 1), j * piece : (j + 1) * piece] = q_all[j][None]
-
-    def w4_copy(k):
-        to = lax.rem(row + k, n_row)
-        return remote(
-            w4_buf.at[row], w4_buf.at[row], w_send.at[n_row + 2 * n_col + k], w4_recv.at[k], (to, col)
-        )
-
-    for k in range(1, n_row):
-        w4_copy(k).start()
-
+    f_copy(row, 0, other).wait_send()
     p_copy(row, 0, other).wait_send()
     for k in range(1, n_y):
+        f_copy(row, k, other).wait_send()
+        f_copy(row, n_y - 1 + k, other).wait_send()
         p_copy(row, k, other).wait_send()
         p_copy(row, n_y - 1 + k, other).wait_send()
 
@@ -451,13 +490,10 @@
         w4_copy(k).wait_send()
 
 
-def hand_over_kernel(a, b, c, a_out, b_out, c_out, sems):
-    pairs = ((a, a_out), (b, b_out), (c, c_out))
-    copies = [pltpu.make_async_copy(src, dst, sems.at[i]) for i, (src, dst) in enumerate(pairs)]
-    for copy in copies:
-        copy.start()
-    for copy in copies:
-        copy.wait()
+def hand_over_kernel(a, b, c, a_out, b_out, c_out):
+    a_out[...] = a[...]
+    b_out[...] = b[...]
+    c_out[...] = c[...]
 
 
 def vmem(n):
@@ -476,10 +512,8 @@
     tiles_dev = nodes // tile
     row_tiles = n_col * tiles_dev
     lanes = pl.cdiv(max(slots, row_tiles), 128) * 128
-    coords = jnp.pad(tile_coords[0, 0].T, ((0, 0), (0, lanes - slots)))
-    degrees = [row_degree.reshape(-1, lanes), col_degree.reshape(-1, lanes)]
-    used = 2 + 2 * degrees[0].shape[0]
-    packed = jnp.pad(jnp.concatenate([coords] + degrees), ((0, -used % 8), (0, 0)))
+    coords = tile_coords[0, 0].T
+    degrees = (row_degree.reshape(-1, lanes), col_degree.reshape(-1, lanes))
 
     quarter = width // n_row
     piece = quarter // n_col
@@ -492,17 +526,19 @@
             shape((width, width), f32),
         ),
         in_specs=[pl.BlockSpec(memory_space=pltpu.SMEM)]
-        + vmem(4)
+        + vmem(6)
         + [pl.BlockSpec(memory_space=pl.ANY)],
         out_specs=tuple(vmem(3)),
         scratch_shapes=[
             pltpu.VMEM((slots, tile, tile), jnp.int32),
             pltpu.VMEM((slots, tile, tile), bf16),
             pltpu.VMEM((8, lanes), jnp.int32),
+            pltpu.VMEM((8, lanes), jnp.int32),
             pltpu.SMEM((8, lanes), jnp.int32),
             pltpu.VMEM((nodes, 1), f32),
             pltpu.VMEM((nodes, 1), f32),
             pltpu.VMEM((n_row,) + block, bf16),
+            pltpu.VMEM((n_row, width, nodes), bf16),
             pltpu.VMEM((n_col,) + block, bf16),
             pltpu.VMEM((tile, width), f32),
             pltpu.VMEM((slots + 1, tile, width), bf16),
@@ -522,6 +558,8 @@
             pltpu.VMEM((n_row, quarter, width), f32),
             dma(()),
             dma(()),
+            dma((2 * n_y,)),
+            dma((n_row,)),
             dma((2 * n_y,)),
             dma((n_row,)),
             dma((2 + n_fast - 1 + 2 * (SLOW - 1) * n_fast,)),
@@ -544,13 +582,12 @@
             collective_id=0, has_side_effects=True, vmem_limit_bytes=56 * MB
         ),
         name="layer",
-    )(tile_live.reshape(-1), packed, features, weight, cotangent, tile_edges[0, 0])
+    )(tile_live.reshape(-1), coords, *degrees, features, weight, cotangent, tile_edges[0, 0])
     return pl.pallas_call(
         hand_over_kernel,
         out_shape=tuple(shape(r.shape, r.dtype) for r in results),
-        in_specs=[pl.BlockSpec(memory_space=pl.ANY)] * 3,
-        out_specs=tuple([pl.BlockSpec(memory_space=pl.ANY)] * 3),
-        scratch_shapes=[dma((3,))],
+        in_specs=vmem(3),
+        out_specs=tuple(vmem(3)),
         compiler_params=pltpu.CompilerParams(vmem_limit_bytes=60 * MB),
         name="hand_over",
     )(*results)

time: 102 us -> 80.3 us (0.79)
  Pallas kernels: 98 us -> 76.3 us
    pallas_call x1, Pallas kernels: 25 us -> 2 us  [shards(): pl.pallas_call(hand_over_kernel, out_shape=tuple((shape(r.shape, r.dtype)...]
    pallas_call x1, Pallas kernels: 73 us -> 74.3 us  [shards(): pl.pallas_call(functools.partial(layer_kernel, n_row, n_col), out_shape=(...]
    reshape x2, local copies, waits for them, and re-layouts: 1.39 us -> 2.54 us  [shards(): degrees = (row_degree.reshape(-1, lanes), col_degree.reshape(-1, lanes))]
where the time goes in v4:
time: 80.3 us; the launch traced here: 80.1 us
  Pallas kernels  76.3 us (95%)
  local copies, waits for them, and re-layouts  2.54 us (3%)
  between operations  1.29 us (2%)
    pallas_call x1, Pallas kernels, shards(): pl.pallas_call(functools.partial(layer_kernel, n_row, n_col), out_shape=(...  74.3 us
    reshape x2, local copies, waits for them, and re-layouts, shards(): degrees = (row_degree.reshape(-1, lanes), col_degree.reshape(-1, lanes))  2.54 us
    pallas_call x1, Pallas kernels, shards(): pl.pallas_call(hand_over_kernel, out_shape=tuple((shape(r.shape, r.dtype)...  2 us

profile of v4, /device:TPU:0, one launch (start us, length us, event | category | flops | bytes accessed | tf_op | source)
XLA Modules:
  0.0 80.1 jit_solution(5013768478698699998)
XLA Ops:
  1.3 1.3 %reshape.16.row_degree = s32[2,256]{1,0:T(2,128)} reshape(s32[512]{0:T(512)} %param.13) | data formatting | bytes 4096 | tf_op jit(solution)/shard_map/reshape | solution.py:516
  2.5 1.3 %reshape.17.col_degree = s32[2,256]{1,0:T(2,128)} reshape(s32[512]{0:T(512)} %param.14) | data formatting | bytes 4096 | tf_op jit(solution)/shard_map/reshape | solution.py:516
  3.8 74.3 %layer.1 = (bf16[512,256]{1,0:T(8,128)(2,1)}, bf16[512,256]{1,0:T(8,128)(2,1)}, f32[256,256]{1,0:T(8,128)}) custom-call(s32[1]{0:T(128)} %bitcast.5.live, s32[2,144]{1,0:T(2,128)} %bitcast.7, s32[2,256]{1,0:T(2,128)} %reshape.16.row_degree, s32[2,256]{1,0:T(2,128)} %reshape.17.col_degree, bf16[512,256]{1,0:T(8,128)(2,1)} %feat.1, bf16[256,256]{1,0:T(8,128)(2,1)} %weight.1, ...), custom_call_target="tpu_custom_call" | custom-call | tf_op jit(solution)/shard_map/layer/pallas_call | solution.py:521
  78.1 2.0 %hand_over.1 = (bf16[512,256]{1,0:T(8,128)(2,1)}, bf16[512,256]{1,0:T(8,128)(2,1)}, f32[256,256]{1,0:T(8,128)}) custom-call(bf16[512,256]{1,0:T(8,128)(2,1)} %get-tuple-element.6.a, bf16[512,256]{1,0:T(8,128)(2,1)} %get-tuple-element.7.b, f32[256,256]{1,0:T(8,128)} %get-tuple-element.8.c), custom_call_target="tpu_custom_call" | custom-call | tf_op jit(solution)/shard_map/hand_over/pallas_call | solution.py:586

commit v5 on v4

--- a/solution.py
+++ b/solution.py
@@ -10,6 +10,7 @@
 MESH = pl.DeviceIdType.MESH
 CORES = 2
 SLOW = 4
+JOIN = 4
 MB = 1024 * 1024
 
 
@@ -35,27 +36,36 @@
     )
 
 
+def groups_of(slots, tiles):
+    return (slots + (JOIN - 1) * tiles) // JOIN
+
+
 def fill_tables(row_tiles, col_tiles, packed, turned, count, slots, tab):
-    lanes = tab.shape[1]
-    coords, coords_t = turned[:slots], packed
+    lanes, wide = packed.shape[1], tab.shape[1]
     s_col = lax.broadcasted_iota(jnp.int32, (slots, 1), 0)
     s_row = lax.broadcasted_iota(jnp.int32, (1, lanes), 1)
-    place = lax.broadcasted_iota(jnp.int32, (slots, lanes), 1)
+    target = lax.broadcasted_iota(jnp.int32, (slots, lanes), 1)
+    place = lax.broadcasted_iota(jnp.int32, (slots, wide), 1)
+    empty = groups_of(slots, row_tiles)
     for half, tiles in ((0, row_tiles), (1, col_tiles)):
-        key_col = jnp.where(s_col < count, coords[:, half : half + 1], tiles)
-        key_row = jnp.where(s_row < count, coords_t[half : half + 1, :], tiles)
+        key_col = jnp.where(s_col < count, turned[:slots, half : half + 1], tiles)
+        key_row = jnp.where(s_row < count, packed[half : half + 1, :], tiles)
         same = (key_row == key_col) & (s_row < s_col)
         earlier = jnp.sum(same.astype(jnp.int32), axis=1, keepdims=True)
-        below = jnp.sum((key_row < key_col).astype(jnp.int32), axis=1, keepdims=True)
-        chosen = ((earlier + below) == place).astype(jnp.int32)
-        source = coords[:, 1 - half : 2 - half]
+        held = jnp.sum((key_col == target).astype(jnp.int32), axis=0, keepdims=True)
+        padded = ((held + (JOIN - 1)) // JOIN) * JOIN
+        begin = jnp.sum(jnp.where(target < key_col, padded, 0), axis=1, keepdims=True)
+        spot = jnp.where(s_col < count, begin + earlier, -1)
+        chosen = (spot == place).astype(jnp.int32)
+        source = turned[:slots, 1 - half : 2 - half]
         follows = (earlier > 0).astype(jnp.int32)
-        upto = jnp.sum((key_col <= place).astype(jnp.int32), axis=0, keepdims=True)
-        here = jnp.sum((key_col == place).astype(jnp.int32), axis=0, keepdims=True)
-        tab[4 * half : 4 * half + 1, :] = jnp.sum(chosen * s_col, axis=0, keepdims=True)
-        tab[4 * half + 1 : 4 * half + 2, :] = jnp.sum(chosen * source, axis=0, keepdims=True)
-        tab[4 * half + 2 : 4 * half + 3, :] = jnp.sum(chosen * follows, axis=0, keepdims=True)
-        tab[4 * half + 3 : 4 * half + 4, :] = jnp.where(here > 0, upto - 1, slots)
+        group = spot // JOIN
+        end = jnp.max(jnp.where(key_col == target, group, -1), axis=0, keepdims=True)
+        base = 4 * half
+        tab[base : base + 1, :] = jnp.sum(chosen * (s_col - slots), axis=0, keepdims=True) + slots
+        tab[base + 1 : base + 2, :] = jnp.sum(chosen * source, axis=0, keepdims=True)
+        tab[base + 2 : base + 3, :] = jnp.sum(chosen * follows, axis=0, keepdims=True)
+        tab[base + 3 : base + 4, :lanes] = jnp.where(end >= 0, end, empty)
 
 
 def layer_kernel(
@@ -82,7 +92,6 @@
     panel,
     turned_feat,
     upstream,
-    acc,
     sums,
     part,
     back,
@@ -128,12 +137,12 @@
     z, x = col // n_fast, lax.rem(col, n_fast)
     f32, bf16 = jnp.float32, jnp.bfloat16
     other = y * CORES + (1 - core)
-    slots, tile = edges.shape[0], edges.shape[1]
+    slots, tile = edges_hbm.shape[0], edges_hbm.shape[1]
     tiles_dev = panel.shape[1]
     nodes, width = feat.shape
     block_shape = (tiles_dev, tile, width)
 
-    load_edges = pltpu.make_async_copy(edges_hbm, edges, e_sem)
+    load_edges = pltpu.make_async_copy(edges_hbm, edges.at[pl.ds(0, slots)], e_sem)
     load_edges.start()
     lanes = row_degree.shape[1]
     parts = nodes // lanes
@@ -217,11 +226,13 @@
     for k in range(1, n_y):
         f_copy(row, k, lax.rem(y + k, n_y) * CORES + core).start()
     f_copy(row, 0, other).start()
+    tab_vmem[...] = jnp.zeros_like(tab_vmem)
     fill_tables(n_col * tiles_dev, n_row * tiles_dev, table, turned, live[0], slots, tab_vmem)
     load_tab = pltpu.make_async_copy(tab_vmem, tab, t_sem)
     load_tab.start()
-    acc[...] = jnp.zeros_like(acc)
-    sums[slots] = jnp.zeros((tile, width), bf16)
+    sums[sums.shape[0] - 1] = jnp.zeros((tile, width), bf16)
+    edges[slots] = jnp.zeros((tile, tile), jnp.int32)
+    turned_edges[slots] = jnp.zeros((tile, tile), bf16)
     for k in range(1, n_y):
         slot = lax.rem(y + k, n_y) * CORES + core
         p_copy(slot, n_y - 1 + k, other).wait_recv()
@@ -233,31 +244,50 @@
     load_edges.wait()
     load_tab.wait()
 
-    unroll = 8 if slots % 16 == 0 else 1
-
-    def products(base, source, flipped, lo, hi):
+    def products(base, source, flipped, count):
+        def step(n, total):
+            keep = tab[base + 2, JOIN * n].astype(f32)
+            mats, vals = [], []
+            for j in range(JOIN):
+                pick, src = tab[base, JOIN * n + j], tab[base + 1, JOIN * n + j]
+                mats.append(turned_edges[pick] if flipped else edges[pick].astype(f32).astype(bf16))
+                vals.append(source[lax.div(src, tiles_dev), lax.rem(src, tiles_dev)])
+            product = jnp.dot(
+                jnp.concatenate(mats, axis=1),
+                jnp.concatenate(vals, axis=0),
+                preferred_element_type=f32,
+            )
+            total = total * keep + product
+            sums[n] = total.astype(bf16)
+            return total
+
+        unroll = max(u for u in range(1, 7) if count % u == 0)
+
+        def body(i, total):
+            for j in range(unroll):
+                total = step(i * unroll + j, total)
+            return total
+
+        lax.fori_loop(0, count // unroll, body, jnp.zeros((tile, width), f32))
+
+    turn_unroll = 8 if slots % 16 == 0 else 1
+
+    def turn(lo, hi):
         def body(i, carry):
-            for j in range(unroll):
-                n = lo + i * unroll + j
-                pick, src = tab[base, n], tab[base + 1, n]
-                keep = tab[base + 2, n].astype(f32)
-                mat = turned_edges[pick] if flipped else edges[pick].astype(f32).astype(bf16)
-                vals = source[lax.div(src, tiles_dev), lax.rem(src, tiles_dev)]
-                total = acc[...] * keep + jnp.dot(mat, vals, preferred_element_type=f32)
-                acc[...] = total
-                sums[n] = total.astype(bf16)
+            for j in range(turn_unroll):
+                n = lo + i * turn_unroll + j
+                turned_edges[n] = jnp.transpose(edges[n].astype(f32)).astype(bf16)
             return carry
 
-        lax.fori_loop(0, (hi - lo) // unroll, body, 0)
+        lax.fori_loop(0, (hi - lo) // turn_unroll, body, 0)
 
     half = slots // 2
-    products(0, panel, False, 0, half)
+    products(0, panel, False, groups_of(slots, n_col * tiles_dev))
     pass_on(2)
     for k in range(1, n_y):
         slot = lax.rem(y + k, n_y) * CORES + core
         f_copy(slot, n_y - 1 + k, other).wait_recv()
         f_copy(slot, n_y - 1 + k, other).start()
-    products(0, panel, False, half, slots)
     for block in range(n_col):
         for j in range(tiles_dev):
             part[block, j] = sums[tab[3, block * tiles_dev + j]]
@@ -279,16 +309,10 @@
         for k in range(1, n_fast):
             x_copy(order[i], k).start()
 
+    turn(0, half)
     for t in range(3, SLOW):
         pass_on(t)
-
-    def turn(i, carry):
-        for j in range(unroll):
-            n = i * unroll + j
-            turned_edges[n] = jnp.transpose(edges[n].astype(f32)).astype(bf16)
-        return carry
-
-    lax.fori_loop(0, slots // unroll, turn, 0)
+    turn(half, slots)
 
     def z_copy(t):
         return remote(
@@ -315,9 +339,8 @@
             slot = t * n_fast + lax.rem(x + k, n_fast)
             up_copy(slot, 0, col).wait_recv()
     start_x(0)
-    products(4, upstream, True, 0, half)
+    products(4, upstream, True, groups_of(slots, n_row * tiles_dev))
     start_x(1)
-    products(4, upstream, True, half, slots)
     for block in range(n_row):
         for j in range(tiles_dev):
             back[block, j] = sums[tab[7, block * tiles_dev + j]]
@@ -512,6 +535,7 @@
     tiles_dev = nodes // tile
     row_tiles = n_col * tiles_dev
     lanes = pl.cdiv(max(slots, row_tiles), 128) * 128
+    wide = pl.cdiv(JOIN * groups_of(slots, row_tiles), 128) * 128
     coords = tile_coords[0, 0].T
     degrees = (row_degree.reshape(-1, lanes), col_degree.reshape(-1, lanes))
 
@@ -530,18 +554,17 @@
         + [pl.BlockSpec(memory_space=pl.ANY)],
         out_specs=tuple(vmem(3)),
         scratch_shapes=[
-            pltpu.VMEM((slots, tile, tile), jnp.int32),
-            pltpu.VMEM((slots, tile, tile), bf16),
+            pltpu.VMEM((slots + 1, tile, tile), jnp.int32),
+            pltpu.VMEM((slots + 1, tile, tile), bf16),
             pltpu.VMEM((8, lanes), jnp.int32),
-            pltpu.VMEM((8, lanes), jnp.int32),
-            pltpu.SMEM((8, lanes), jnp.int32),
+            pltpu.VMEM((8, wide), jnp.int32),
+            pltpu.SMEM((8, wide), jnp.int32),
             pltpu.VMEM((nodes, 1), f32),
             pltpu.VMEM((nodes, 1), f32),
             pltpu.VMEM((n_row,) + block, bf16),
             pltpu.VMEM((n_row, width, nodes), bf16),
             pltpu.VMEM((n_col,) + block, bf16),
-            pltpu.VMEM((tile, width), f32),
-            pltpu.VMEM((slots + 1, tile, width), bf16),
+            pltpu.VMEM((groups_of(slots, row_tiles) + 1, tile, width), bf16),
             pltpu.VMEM((n_col,) + block, bf16),
             pltpu.VMEM((n_row,) + block, bf16),
             pltpu.VMEM((SLOW * (n_fast - 1),) + block, bf16),

time: 80.3 us -> 78.2 us (0.974)
  Pallas kernels: 76.3 us -> 74.2 us
    pallas_call x1, Pallas kernels: 74.3 us -> 72.2 us  [shards(): pl.pallas_call(functools.partial(layer_kernel, n_row, n_col), out_shape=(...]
where the time goes in v5:
time: 78.2 us; the launch traced here: 78 us
  Pallas kernels  74.2 us (95%)
  local copies, waits for them, and re-layouts  2.54 us (3%)
  between operations  1.29 us (2%)
    pallas_call x1, Pallas kernels, shards(): pl.pallas_call(functools.partial(layer_kernel, n_row, n_col), out_shape=(...  72.2 us
    reshape x2, local copies, waits for them, and re-layouts, shards(): degrees = (row_degree.reshape(-1, lanes), col_degree.reshape(-1, lanes))  2.54 us
    pallas_call x1, Pallas kernels, shards(): pl.pallas_call(hand_over_kernel, out_shape=tuple((shape(r.shape, r.dtype)...  2 us

profile of v5, /device:TPU:0, one launch (start us, length us, event | category | flops | bytes accessed | tf_op | source)
XLA Modules:
  0.0 78.0 jit_solution(10113991448597465359)
XLA Ops:
  1.3 1.3 %reshape.16.row_degree = s32[2,256]{1,0:T(2,128)} reshape(s32[512]{0:T(512)} %param.13) | data formatting | bytes 4096 | tf_op jit(solution)/shard_map/reshape | solution.py:540
  2.5 1.3 %reshape.17.col_degree = s32[2,256]{1,0:T(2,128)} reshape(s32[512]{0:T(512)} %param.14) | data formatting | bytes 4096 | tf_op jit(solution)/shard_map/reshape | solution.py:540
  3.8 72.2 %layer.1 = (bf16[512,256]{1,0:T(8,128)(2,1)}, bf16[512,256]{1,0:T(8,128)(2,1)}, f32[256,256]{1,0:T(8,128)}) custom-call(s32[1]{0:T(128)} %bitcast.5.live, s32[2,144]{1,0:T(2,128)} %bitcast.7, s32[2,256]{1,0:T(2,128)} %reshape.16.row_degree, s32[2,256]{1,0:T(2,128)} %reshape.17.col_degree, bf16[512,256]{1,0:T(8,128)(2,1)} %feat.1, bf16[256,256]{1,0:T(8,128)(2,1)} %weight.1, ...), custom_call_target="tpu_custom_call" | custom-call | tf_op jit(solution)/shard_map/layer/pallas_call | solution.py:545
  76.0 2.0 %hand_over.1 = (bf16[512,256]{1,0:T(8,128)(2,1)}, bf16[512,256]{1,0:T(8,128)(2,1)}, f32[256,256]{1,0:T(8,128)}) custom-call(bf16[512,256]{1,0:T(8,128)(2,1)} %get-tuple-element.6.a, bf16[512,256]{1,0:T(8,128)(2,1)} %get-tuple-element.7.b, f32[256,256]{1,0:T(8,128)} %get-tuple-element.8.c), custom_call_target="tpu_custom_call" | custom-call | tf_op jit(solution)/shard_map/hand_over/pallas_call | solution.py:609

commit v6 on v5

--- a/solution.py
+++ b/solution.py
@@ -95,6 +95,10 @@
     sums,
     part,
     back,
+    f1_buf,
+    f2_out,
+    f2_buf,
+    first_sum,
     x_buf,
     z_out,
     z_buf,
@@ -115,6 +119,10 @@
     f_recv,
     u_send,
     u_recv,
+    f1_send,
+    f1_recv,
+    f2_send,
+    f2_recv,
     x_send,
     x_recv,
     z_send,
@@ -144,12 +152,13 @@
 
     load_edges = pltpu.make_async_copy(edges_hbm, edges.at[pl.ds(0, slots)], e_sem)
     load_edges.start()
-    lanes = row_degree.shape[1]
+    lanes = packed.shape[1]
     parts = nodes // lanes
     packed[...] = jnp.zeros_like(packed)
     packed[0:2, :slots] = coords[...]
-    packed[2 : 2 + parts] = row_degree[...]
-    packed[2 + parts : 2 + 2 * parts] = col_degree[...]
+    for h in range(parts):
+        packed[2 + h, :] = row_degree[pl.ds(h * lanes, lanes)]
+        packed[2 + parts + h, :] = col_degree[pl.ds(h * lanes, lanes)]
     table = packed[...]
     turned = jnp.transpose(table)
     for h in range(parts):
@@ -297,7 +306,7 @@
         block = lax.rem(z + t, SLOW) * n_fast + to
         slot = t * (n_fast - 1) + k - 1
         return remote(
-            part.at[block], x_buf.at[slot], x_send.at[slot], x_recv.at[slot], (row, z * n_fast + to)
+            part.at[block, 1:], x_buf.at[slot], x_send.at[slot], x_recv.at[slot], (row, z * n_fast + to)
         )
 
     order = (2, 3, 1, 0)
@@ -312,7 +321,39 @@
     turn(0, half)
     for t in range(3, SLOW):
         pass_on(t)
+
+    def f1_copy(t, k):
+        slot = t * n_fast + k
+        block = lax.rem(z + t, SLOW) * n_fast + lax.rem(x + k, n_fast)
+        return remote(
+            part.at[block, 0],
+            f1_buf.at[slot],
+            f1_send.at[slot],
+            f1_recv.at[slot],
+            (row, lax.rem(z + t, SLOW) * n_fast + x),
+        )
+
+    for t in order[:3]:
+        for k in range(n_fast):
+            f1_copy(t, k).start()
     turn(half, slots)
+
+    def f2_copy(k):
+        to = z * n_fast + lax.rem(x + k, n_fast)
+        return remote(f2_out.at[k], f2_buf.at[k], f2_send.at[k], f2_recv.at[k], (row, to))
+
+    def merge_f1():
+        for k in reversed(range(n_fast)):
+            block = z * n_fast + lax.rem(x + k, n_fast)
+            total = part[pl.ds(block, 1), 0][0].astype(f32)
+            for t in order[:3]:
+                f1_copy(t, k).wait_recv()
+                total = total + f1_buf[t * n_fast + k].astype(f32)
+            if k:
+                f2_out[k] = total.astype(bf16)
+                f2_copy(k).start()
+            else:
+                first_sum[...] = total
 
     def z_copy(t):
         return remote(
@@ -326,7 +367,7 @@
     def merge_x(i):
         t = order[i]
         block = lax.rem(z + t, SLOW) * n_fast + x
-        total = part[pl.ds(block, 1)][0].astype(f32)
+        total = part[pl.ds(block, 1), 1:][0].astype(f32)
         for k in range(1, n_fast):
             x_copy(t, k).wait_recv()
             total = total + x_buf[t * (n_fast - 1) + k - 1].astype(f32)
@@ -408,6 +449,8 @@
 
     merge_x(1)
     start_x(3)
+    merge_f1()
+    merge_x(2)
 
     total = y_out[0].astype(f32)
     for k in range(1, n_y):
@@ -433,7 +476,7 @@
     for k in range(1, n_col):
         w3_copy(k).start()
 
-    merge_x(2)
+    merge_x(3)
 
     for k in range(1, n_col):
         w3_copy(k).wait_recv()
@@ -449,13 +492,17 @@
     for k in range(1, n_row):
         w4_copy(k).start()
 
-    merge_x(3)
-
     total = z_out[0].astype(f32)
     for t in order[:3]:
         z_copy(t).wait_recv()
         total = total + z_buf[t].astype(f32)
-    out[...] = (row_scale[...] * total.reshape((nodes, width))).astype(bf16)
+    rest_scale = row_scale[tile:, :]
+    out[tile:, :] = (rest_scale * total.reshape((nodes - tile, width))).astype(bf16)
+    total = first_sum[...]
+    for k in range(1, n_fast):
+        f2_copy(k).wait_recv()
+        total = total + f2_buf[k].astype(f32)
+    out[:tile, :] = (row_scale[:tile, :] * total).astype(bf16)
 
     f_copy(row, 0, other).wait_send()
     p_copy(row, 0, other).wait_send()
@@ -499,6 +546,10 @@
             x_copy(t, k).wait_send()
     for t in order[:3]:
         z_copy(t).wait_send()
+        for k in range(n_fast):
+            f1_copy(t, k).wait_send()
+    for k in range(1, n_fast):
+        f2_copy(k).wait_send()
     for k in range(1, n_row):
         w1_copy(k).wait_send()
     for k in range(1, n_col):
@@ -537,11 +588,11 @@
     lanes = pl.cdiv(max(slots, row_tiles), 128) * 128
     wide = pl.cdiv(JOIN * groups_of(slots, row_tiles), 128) * 128
     coords = tile_coords[0, 0].T
-    degrees = (row_degree.reshape(-1, lanes), col_degree.reshape(-1, lanes))
 
     quarter = width // n_row
     piece = quarter // n_col
     block = (tiles_dev, tile, width)
+    rest = (tiles_dev - 1, tile, width)
     results = pl.pallas_call(
         functools.partial(layer_kernel, n_row, n_col),
         out_shape=(
@@ -567,9 +618,13 @@
             pltpu.VMEM((groups_of(slots, row_tiles) + 1, tile, width), bf16),
             pltpu.VMEM((n_col,) + block, bf16),
             pltpu.VMEM((n_row,) + block, bf16),
-            pltpu.VMEM((SLOW * (n_fast - 1),) + block, bf16),
-            pltpu.VMEM((SLOW,) + block, bf16),
-            pltpu.VMEM((SLOW,) + block, bf16),
+            pltpu.VMEM((SLOW * n_fast, tile, width), bf16),
+            pltpu.VMEM((n_fast, tile, width), bf16),
+            pltpu.VMEM((n_fast, tile, width), bf16),
+            pltpu.VMEM((tile, width), f32),
+            pltpu.VMEM((SLOW * (n_fast - 1),) + rest, bf16),
+            pltpu.VMEM((SLOW,) + rest, bf16),
+            pltpu.VMEM((SLOW,) + rest, bf16),
             pltpu.VMEM((n_y,) + block, bf16),
             pltpu.VMEM((n_y,) + block, bf16),
             pltpu.VMEM((n_y,) + block, bf16),
@@ -587,6 +642,10 @@
             dma((n_row,)),
             dma((2 + n_fast - 1 + 2 * (SLOW - 1) * n_fast,)),
             dma((n_col,)),
+            dma((SLOW * n_fast,)),
+            dma((SLOW * n_fast,)),
+            dma((n_fast,)),
+            dma((n_fast,)),
             dma((SLOW * (n_fast - 1),)),
             dma((SLOW * (n_fast - 1),)),
             dma((SLOW,)),
@@ -605,7 +664,7 @@
             collective_id=0, has_side_effects=True, vmem_limit_bytes=56 * MB
         ),
         name="layer",
-    )(tile_live.reshape(-1), coords, *degrees, features, weight, cotangent, tile_edges[0, 0])
+    )(tile_live.reshape(-1), coords, row_degree, col_degree, features, weight, cotangent, tile_edges[0, 0])
     return pl.pallas_call(
         hand_over_kernel,
         out_shape=tuple(shape(r.shape, r.dtype) for r in results),

time: 78.2 us -> 71.9 us (0.919)
  Pallas kernels: 74.2 us -> 69.7 us
  local copies, waits for them, and re-layouts: 2.54 us -> 0 us
    pallas_call x1, Pallas kernels: 72.2 us -> 67.7 us  [shards(): pl.pallas_call(functools.partial(layer_kernel, n_row, n_col), out_shape=(...]
    reshape x2 -> x0, local copies, waits for them, and re-layouts: 2.54 us -> none  [shards(): degrees = (row_degree.reshape(-1, lanes), col_degree.reshape(-1, lanes))]
where the time goes in v6:
time: 71.9 us; the launch traced here: 71 us
  Pallas kernels  69.7 us (97%)
  between operations  1.29 us (2%)
    pallas_call x1, Pallas kernels, shards(): pl.pallas_call(functools.partial(layer_kernel, n_row, n_col), out_shape=(...  67.7 us
    pallas_call x1, Pallas kernels, shards(): pl.pallas_call(hand_over_kernel, out_shape=tuple((shape(r.shape, r.dtype)...  2 us

profile of v6, /device:TPU:0, one launch (start us, length us, event | category | flops | bytes accessed | tf_op | source)
XLA Modules:
  0.0 71.0 jit_solution(11449860504077527733)
XLA Ops:
  1.3 67.7 %layer.1 = (bf16[512,256]{1,0:T(8,128)(2,1)}, bf16[512,256]{1,0:T(8,128)(2,1)}, f32[256,256]{1,0:T(8,128)}) custom-call(s32[1]{0:T(128)} %bitcast.5.live, s32[2,144]{1,0:T(2,128)} %bitcast.7, s32[512]{0:T(512)} %row_degree.1, s32[512]{0:T(512)} %col_degree.1, bf16[512,256]{1,0:T(8,128)(2,1)} %feat.1, bf16[256,256]{1,0:T(8,128)(2,1)} %weight.1, ...), custom_call_target="tpu_custom_call" | custom-call | tf_op jit(solution)/shard_map/layer/pallas_call | solution.py:596
  69.0 2.0 %hand_over.1 = (bf16[512,256]{1,0:T(8,128)(2,1)}, bf16[512,256]{1,0:T(8,128)(2,1)}, f32[256,256]{1,0:T(8,128)}) custom-call(bf16[512,256]{1,0:T(8,128)(2,1)} %get-tuple-element.6.a, bf16[512,256]{1,0:T(8,128)(2,1)} %get-tuple-element.7.b, f32[256,256]{1,0:T(8,128)} %get-tuple-element.8.c), custom_call_target="tpu_custom_call" | custom-call | tf_op jit(solution)/shard_map/hand_over/pallas_call | solution.py:668

commit v7 on v6

--- a/solution.py
+++ b/solution.py
@@ -110,6 +110,7 @@
     q_out,
     w2_buf,
     q_all,
+    w_stage,
     w4_buf,
     e_sem,
     t_sem,
@@ -404,7 +405,7 @@
             turned_feat[block], back[block].reshape((nodes, width)), preferred_element_type=f32
         )
     for r in range(n_row):
-        w_out[r] = terms[r * quarter : (r + 1) * quarter]
+        w_out[r] = terms[r * quarter : (r + 1) * quarter].astype(bf16)
 
     def w1_copy(k):
         to = lax.rem(row + k, n_row)
@@ -433,10 +434,10 @@
     merge_x(0)
     start_x(2)
 
-    total = w_out[pl.ds(row, 1)][0]
+    total = w_out[pl.ds(row, 1)][0].astype(f32)
     for k in range(1, n_row):
         w1_copy(k).wait_recv()
-        total = total + w1_buf[k]
+        total = total + w1_buf[k].astype(f32)
     for j in range(n_col):
         q_out[j] = total[j * piece : (j + 1) * piece]
 
@@ -481,7 +482,8 @@
     for k in range(1, n_col):
         w3_copy(k).wait_recv()
     for j in range(n_col):
-        w4_buf[pl.ds(row, 1), j * piece : (j + 1) * piece] = q_all[j][None]
+        w_stage[j * piece : (j + 1) * piece] = q_all[j]
+    w4_buf[pl.ds(row, 1)] = w_stage[...].astype(bf16)[None]
 
     def w4_copy(k):
         to = lax.rem(row + k, n_row)
@@ -559,7 +561,7 @@
     for k in range(1, n_row):
         w4_copy(k).wait_recv()
     for r in range(n_row):
-        grad_weight[r * quarter : (r + 1) * quarter] = w4_buf[r]
+        grad_weight[r * quarter : (r + 1) * quarter] = w4_buf[r].astype(f32)
     for k in range(1, n_row):
         w4_copy(k).wait_send()
 
@@ -628,12 +630,13 @@
             pltpu.VMEM((n_y,) + block, bf16),
             pltpu.VMEM((n_y,) + block, bf16),
             pltpu.VMEM((n_y,) + block, bf16),
-            pltpu.VMEM((n_row, quarter, width), f32),
-            pltpu.VMEM((n_row, quarter, width), f32),
+            pltpu.VMEM((n_row, quarter, width), bf16),
+            pltpu.VMEM((n_row, quarter, width), bf16),
             pltpu.VMEM((n_col, piece, width), f32),
             pltpu.VMEM((n_col, piece, width), f32),
             pltpu.VMEM((n_col, piece, width), f32),
-            pltpu.VMEM((n_row, quarter, width), f32),
+            pltpu.VMEM((quarter, width), f32),
+            pltpu.VMEM((n_row, quarter, width), bf16),
             dma(()),
             dma(()),
             dma((2 * n_y,)),

time: 71.9 us -> 70.4 us (0.979)
  Pallas kernels: 69.7 us -> 68.9 us
    pallas_call x1, Pallas kernels: 67.7 us -> 66.9 us  [shards(): pl.pallas_call(functools.partial(layer_kernel, n_row, n_col), out_shape=(...]
where the time goes in v7:
time: 70.4 us; the launch traced here: 70.2 us
  Pallas kernels  68.9 us (98%)
  between operations  1.29 us (2%)
    pallas_call x1, Pallas kernels, shards(): pl.pallas_call(functools.partial(layer_kernel, n_row, n_col), out_shape=(...  66.9 us
    pallas_call x1, Pallas kernels, shards(): pl.pallas_call(hand_over_kernel, out_shape=tuple((shape(r.shape, r.dtype)...  2 us

profile of v7, /device:TPU:0, one launch (start us, length us, event | category | flops | bytes accessed | tf_op | source)
XLA Modules:
  0.0 70.2 jit_solution(11100623971119833599)
XLA Ops:
  1.3 66.9 %layer.1 = (bf16[512,256]{1,0:T(8,128)(2,1)}, bf16[512,256]{1,0:T(8,128)(2,1)}, f32[256,256]{1,0:T(8,128)}) custom-call(s32[1]{0:T(128)} %bitcast.5.live, s32[2,144]{1,0:T(2,128)} %bitcast.7, s32[512]{0:T(512)} %row_degree.1, s32[512]{0:T(512)} %col_degree.1, bf16[512,256]{1,0:T(8,128)(2,1)} %feat.1, bf16[256,256]{1,0:T(8,128)(2,1)} %weight.1, ...), custom_call_target="tpu_custom_call" | custom-call | tf_op jit(solution)/shard_map/layer/pallas_call | solution.py:598
  68.2 2.0 %hand_over.1 = (bf16[512,256]{1,0:T(8,128)(2,1)}, bf16[512,256]{1,0:T(8,128)(2,1)}, f32[256,256]{1,0:T(8,128)}) custom-call(bf16[512,256]{1,0:T(8,128)(2,1)} %get-tuple-element.6.a, bf16[512,256]{1,0:T(8,128)(2,1)} %get-tuple-element.7.b, f32[256,256]{1,0:T(8,128)} %get-tuple-element.8.c), custom_call_target="tpu_custom_call" | custom-call | tf_op jit(solution)/shard_map/hand_over/pallas_call | solution.py:671
